TPU v7x, 256 devices: a whole 4x4x8 slice. The times are simulated.
256 devices in a mesh: patch: 64 (over y, z, core), sample: 4 (over x).
Axes of the slice: x: 4, y: 4, z: 8, core: 2. Of those that a mesh axis runs over, the one named last changes fastest.
Arguments:
- edge_latents: bfloat16 [4, 65536, 512], P('sample', 'patch'), may hold values from -6 to 6
- node_latents: bfloat16 [4, 16384, 512], P('sample', 'patch'), may hold values from -6 to 6
- edge_cotangent: bfloat16 [4, 65536, 512], P('sample', 'patch'), may hold values from -6 to 6
- node_cotangent: bfloat16 [4, 16384, 512], P('sample', 'patch'), may hold values from -6 to 6
- senders: int32 [65536], P('patch'), may hold values from 0 to 575, as said below
- receivers: int32 [65536], P('patch'), may hold values from 0 to 255
- send_rows: int32 [4096, 4], P('patch'), may hold values from 0 to 255
- edge_first: bfloat16 [1536, 512], replicated, may hold values from -0.15625 to 0.15625
- edge_second: bfloat16 [512, 512], replicated, may hold values from -0.25 to 0.25
- edge_gain: float32 [512], replicated, may hold values from 0.25 to 1.75
- node_first: bfloat16 [1024, 512], replicated, may hold values from -0.1875 to 0.1875
- node_second: bfloat16 [512, 512], replicated, may hold values from -0.25 to 0.25
- node_gain: float32 [512], replicated, may hold values from 0.25 to 1.75
Outputs:
- edge_grad: bfloat16 [4, 65536, 512], P('sample', 'patch')
- node_grad: bfloat16 [4, 16384, 512], P('sample', 'patch')
- edge_first_grad: bfloat16 [1536, 512], replicated
- edge_second_grad: bfloat16 [512, 512], replicated
- node_first_grad: bfloat16 [1024, 512], replicated
- node_second_grad: bfloat16 [512, 512], replicated
- edge_gain_grad: bfloat16 [512], replicated
- node_gain_grad: bfloat16 [512], replicated
Inputs may be any that keep to these rules, and one draw needn't show every extreme that they name: `senders`: each patch's sender table has 576 rows: the last 32 nodes of the patch before it (cyclically), its own 256 nodes, the first 32 nodes of the patch after it, then 4 rows from each patch in order.
All inputs are finite; a program needn't handle non-finite values.
Results may differ from a plain program's by a relative error of at most 0.012.
Values may be sent and summed in bfloat16 or wider, within the bound.
A program may use at most 128 MiB of HBM per device.

v0:
```python
import jax
import jax.numpy as jnp
from jax import lax
from jax.sharding import PartitionSpec as P

RIM = 32
FAR = 4


def with_halo(cells, sides, width):
    for axis, dim in sides:
        count = lax.axis_size(axis)
        head = lax.slice_in_dim(cells, 0, width, axis=dim)
        tail = lax.slice_in_dim(cells, cells.shape[dim] - width, cells.shape[dim], axis=dim)
        cells = jnp.concatenate(
            [
                lax.ppermute(tail, axis, [(i, (i + 1) % count) for i in range(count)]),
                cells,
                lax.ppermute(head, axis, [((i + 1) % count, i) for i in range(count)]),
            ],
            axis=dim,
        )
    return cells


def from_behind(array, axis, by):
    size = lax.axis_size(axis)
    return lax.ppermute(array, axis, [(i, (i + by) % size) for i in range(size)])


def normalize(values):
    center = values - jnp.mean(values, axis=1, keepdims=True)
    spread = jnp.mean(center * center, axis=1, keepdims=True)
    scale = lax.rsqrt(spread + 1e-05)
    return (center * scale, scale)


def normalize_back(grads, normed, scale):
    first = jnp.mean(grads, axis=1, keepdims=True)
    second = jnp.mean(grads * normed, axis=1, keepdims=True)
    return (grads - first - normed * second) * scale


def layer_backward(
    edges_in,
    sent_latent,
    nodes_in,
    recv_ids,
    edge_cot,
    node_cot,
    edge_first,
    edge_second,
    edge_gain,
    node_first,
    node_second,
    node_gain,
):
    width = nodes_in.shape[1]
    recv_latent = nodes_in[recv_ids]
    edge_input = jnp.concatenate([edges_in, sent_latent, recv_latent], axis=1)
    edge_pre = jnp.dot(edge_input, edge_first, preferred_element_type=jnp.float32)
    edge_sig = jax.nn.sigmoid(edge_pre)
    edge_act = (edge_pre * edge_sig).astype(jnp.bfloat16)
    edge_raw = jnp.dot(edge_act, edge_second, preferred_element_type=jnp.float32)
    edge_hat, edge_scale = normalize(edge_raw)
    update = edge_hat * edge_gain
    inflow = jax.ops.segment_sum(update, recv_ids, num_segments=nodes_in.shape[0]).astype(
        jnp.bfloat16
    )
    node_input = jnp.concatenate([nodes_in, inflow], axis=1)
    node_pre = jnp.dot(node_input, node_first, preferred_element_type=jnp.float32)
    node_sig = jax.nn.sigmoid(node_pre)
    node_act = (node_pre * node_sig).astype(jnp.bfloat16)
    node_raw = jnp.dot(node_act, node_second, preferred_element_type=jnp.float32)
    node_hat, node_scale = normalize(node_raw)
    node_upstream = node_cot.astype(jnp.float32)
    node_gain_grad = jnp.sum(node_upstream * node_hat, axis=0)
    node_raw_grad = normalize_back(node_upstream * node_gain, node_hat, node_scale).astype(
        jnp.bfloat16
    )
    node_second_grad = jnp.dot(node_act.T, node_raw_grad, preferred_element_type=jnp.float32)
    node_act_grad = jnp.dot(node_raw_grad, node_second.T, preferred_element_type=jnp.float32)
    node_pre_grad = (node_act_grad * node_sig * (1.0 + node_pre * (1.0 - node_sig))).astype(
        jnp.bfloat16
    )
    node_first_grad = jnp.dot(node_input.T, node_pre_grad, preferred_element_type=jnp.float32)
    node_input_grad = jnp.dot(node_pre_grad, node_first.T, preferred_element_type=jnp.float32)
    update_grad = edge_cot.astype(jnp.float32) + node_input_grad[:, width:][recv_ids]
    edge_gain_grad = jnp.sum(update_grad * edge_hat, axis=0)
    edge_raw_grad = normalize_back(update_grad * edge_gain, edge_hat, edge_scale).astype(
        jnp.bfloat16
    )
    edge_second_grad = jnp.dot(edge_act.T, edge_raw_grad, preferred_element_type=jnp.float32)
    edge_act_grad = jnp.dot(edge_raw_grad, edge_second.T, preferred_element_type=jnp.float32)
    edge_pre_grad = (edge_act_grad * edge_sig * (1.0 + edge_pre * (1.0 - edge_sig))).astype(
        jnp.bfloat16
    )
    edge_first_grad = jnp.dot(edge_input.T, edge_pre_grad, preferred_element_type=jnp.float32)
    edge_input_grad = jnp.dot(edge_pre_grad, edge_first.T, preferred_element_type=jnp.float32)
    edge_grad = (edge_cot.astype(jnp.float32) + edge_input_grad[:, :width]).astype(jnp.bfloat16)
    sent_grad = edge_input_grad[:, width : 2 * width]
    node_partial = (
        node_upstream
        + node_input_grad[:, :width]
        + jax.ops.segment_sum(
            edge_input_grad[:, 2 * width :], recv_ids, num_segments=nodes_in.shape[0]
        )
    )
    weight_terms = (
        edge_first_grad,
        edge_second_grad,
        node_first_grad,
        node_second_grad,
        edge_gain_grad,
        node_gain_grad,
    )
    return (edge_grad, sent_grad, node_partial, weight_terms)


def on_device(
    edge_latents,
    node_latents,
    edge_cotangent,
    node_cotangent,
    senders,
    receivers,
    send_rows,
    edge_first,
    edge_second,
    edge_gain,
    node_first,
    node_second,
    node_gain,
):
    patches = lax.axis_size("patch")
    own_nodes = node_latents[0]
    count = own_nodes.shape[0]
    width = own_nodes.shape[1]
    extended = with_halo(own_nodes, (("patch", 0),), RIM)
    outgoing = own_nodes[send_rows]
    incoming = lax.all_to_all(outgoing, "patch", split_axis=0, concat_axis=0, tiled=True)
    table = jnp.concatenate([extended, incoming.reshape(patches * FAR, width)], axis=0)
    edge_grad, sent_grad, node_partial, weight_terms = layer_backward(
        edge_latents[0],
        table[senders],
        own_nodes,
        receivers,
        edge_cotangent[0],
        node_cotangent[0],
        edge_first,
        edge_second,
        edge_gain,
        node_first,
        node_second,
        node_gain,
    )
    table_grad = jax.ops.segment_sum(sent_grad, senders, num_segments=table.shape[0])
    from_next = from_behind(table_grad[:RIM].astype(jnp.bfloat16), "patch", -1).astype(jnp.float32)
    from_prev = from_behind(
        table_grad[RIM + count : 2 * RIM + count].astype(jnp.bfloat16), "patch", 1
    ).astype(jnp.float32)
    far_grad = table_grad[2 * RIM + count :].reshape(patches, FAR, width)
    returned = lax.all_to_all(
        far_grad.astype(jnp.bfloat16), "patch", split_axis=0, concat_axis=0, tiled=True
    ).astype(far_grad.dtype)
    node_total = node_partial + table_grad[RIM : RIM + count]
    node_total = node_total + jnp.pad(from_prev, ((0, count - RIM), (0, 0)))
    node_total = node_total + jnp.pad(from_next, ((count - RIM, 0), (0, 0)))
    node_total = node_total + jax.ops.segment_sum(
        returned.reshape(patches * FAR, width), send_rows.reshape(-1), num_segments=count
    )
    summed = lax.psum(
        (
            weight_terms[0],
            weight_terms[1],
            weight_terms[2],
            weight_terms[3],
            weight_terms[4],
            weight_terms[5],
        ),
        ("patch", "sample"),
    )
    finals = tuple((term.astype(jnp.bfloat16) for term in summed))
    return (
        edge_grad[None],
        node_total.astype(jnp.bfloat16)[None],
        finals[0],
        finals[1],
        finals[2],
        finals[3],
        finals[4],
        finals[5],
    )


def solution(mesh):
    return jax.shard_map(
        on_device,
        mesh=mesh,
        in_specs=(
            P("sample", "patch", None),
            P("sample", "patch", None),
            P("sample", "patch", None),
            P("sample", "patch", None),
            P("patch"),
            P("patch"),
            P("patch", None),
            P(),
            P(),
            P(),
            P(),
            P(),
            P(),
        ),
        out_specs=(
            P("sample", "patch", None),
            P("sample", "patch", None),
            P(),
            P(),
            P(),
            P(),
            P(),
            P(),
        ),
        check_vma=False,
    )
```

profile of v0, /device:TPU:1, one launch (start us, length us, event | category | flops | bytes accessed | tf_op | source)
XLA Modules:
  0.0 274.4 jit_solution(2588927336006680791)
XLA Ops:
  0.6 0.0 copy-start
  0.7 0.0 copy-start.1
  0.7 0.8 compare_select_fusion.2
  1.5 0.1 copy.26
  1.6 0.1 reshape.84
  1.7 2.2 gather_fusion
  3.9 0.8 reshape.83
  4.7 13.2 %all-to-all-start = ((bf16[64,4,512]{2,1,0:T(4,128)(2,1)}), bf16[64,4,512]{2,1,0:T(4,128)(2,1)S(1)}, u32[]{:S(2)}, u32[]{:S(2)}) async-start(bf16[64,4,512]{2,1,0:T(4,128)(2,1)} %reshape.83), calls=%async_computation | async-start | bytes 524288 | tf_op jit(solution)/shard_map/all_to_all | solution.py:141
  17.9 1.7 collective-permute-start
  19.6 0.1 copy.30
  19.7 0.6 reshape.140
  20.4 1.5 copy.25
  21.9 5.1 %gather_fusion.2 = bf16[1024,512]{1,0:T(8,128)(2,1)} fusion(bf16[256,512]{1,0:T(8,128)(2,1)S(1)} %bitcast.48, s32[1024]{0:T(1024)S(1)} %fusion.31), kind=kCustom, calls=%fused_computation.2 | custom fusion | bytes 2101248 | tf_op jit(solution)/shard_map/gather | solution.py:59
  26.9 3.2 %all-to-all-done = bf16[64,4,512]{2,1,0:T(4,128)(2,1)S(1)} async-done(((bf16[64,4,512]{2,1,0:T(4,128)(2,1)}), bf16[64,4,512]{2,1,0:T(4,128)(2,1)S(1)}, u32[]{:S(2)}, u32[]{:S(2)}) %all-to-all-start) | async-done | bytes 262176 | tf_op jit(solution)/shard_map/all_to_all | solution.py:141
  30.1 0.8 reshape.75
  30.9 1.0 pad_maximum_fusion.3
  31.9 5.1 %gather_fusion.1 = bf16[1024,512]{1,0:T(8,128)(2,1)} fusion(bf16[576,512]{1,0:T(8,128)(2,1)S(1)} %pad_maximum_fusion.3, s32[1024]{0:T(1024)S(1)} %fusion.30), kind=kCustom, calls=%fused_computation.1 | custom fusion | bytes 2101248 | tf_op jit(solution)/shard_map/gather | solution.py:145
  37.0 5.3 %multiply_convert_fusion.2 = (bf16[1024,512]{1,0:T(8,128)(2,1)S(1)}, f32[1024,512]{1,0:T(8,128)}) fusion(bf16[1536,512]{1,0:T(8,128)(2,1)S(1)} %copy-done, bf16[1024,512]{1,0:T(8,128)(2,1)} %gather_fusion.2, bf16[1024,512]{1,0:T(8,128)(2,1)} %gather_fusion.1, bf16[1024,512]{1,0:T(8,128)(2,1)} %bitcast.52), kind=kOutput, calls=%fused_computation.21 | convolution fusion | flops 1622671360 | bytes 7864320 | tf_op jit(solution)/shard_map/dot_general | solution.py:61
  42.3 0.8 fusion.41
  43.1 0.3 multiply_reduce_fusion.2
  43.4 1.0 copy-done.2
  44.3 1.6 fusion.5
  45.9 2.9 %copy.27 = f32[1024,512]{1,0:T(8,128)} copy(f32[1024,512]{0,1:T(8,128)} %fusion.5) | data formatting | bytes 4194304 | tf_op jit(solution)/shard_map/mul | solution.py:66
  48.8 7.6 %scatter_custom_fusion = f32[256,512]{1,0:T(8,128)S(1)} fusion(s32[1024]{0:T(1024)S(1)} %copy-done.18, f32[1024,512]{1,0:T(8,128)} %copy.27, f32[]{:T(128)} %constant.10.clone.1), kind=kCustom, calls=%fused_computation.59 | custom fusion | flops 524288 | bytes 524800 | tf_op jit(solution)/shard_map/scatter-add | solution.py:67
  56.4 0.0 copy-start.21
  56.5 1.7 fusion.24
  58.2 0.0 copy-start.12
  58.2 0.0 copy-start.19
  58.2 0.4 fusion.42
  58.6 0.2 multiply_reduce_fusion.4
  58.8 0.3 copy-done.12
  59.1 0.3 fusion.22
  59.5 0.5 fusion.9
  60.0 0.0 copy-start.9
  60.0 1.6 fusion.36
  61.6 0.5 fusion.43
  62.0 1.8 fusion.23
  63.9 4.9 %gather_fusion.3 = f32[1024,512]{1,0:T(8,128)} fusion(f32[256,512]{1,0:T(8,128)S(1)} %slice.63, s32[1024]{0:T(1024)S(1)} %fusion.31), kind=kCustom, calls=%fused_computation.3 | custom fusion | bytes 4198400 | tf_op jit(solution)/shard_map/gather | solution.py:88
  68.8 2.9 %copy.28 = f32[1024,512]{0,1:T(8,128)} copy(f32[1024,512]{1,0:T(8,128)} %gather_fusion.3) | data formatting | bytes 4194304 | tf_op jit(solution)/shard_map/gather | solution.py:88
  71.7 3.2 %multiply_reduce_fusion = (f32[512]{0:T(512)S(1)}, f32[1024]{0:T(1024)S(1)}, f32[1024]{0:T(1024)S(1)}) fusion(f32[1024,512]{0,1:T(8,128)} %copy-done.2, f32[1024]{0:T(1024)S(1)} %add_rsqrt_fusion, f32[1024]{0:T(1024)S(1)} %broadcast_multiply_fusion.2, f32[1024,512]{0,1:T(8,128)} %copy.28, bf16[1,1024,512]{1,2,0:T(8,128)(2,1)S(1)} %copy.25, f32[512]{0:T(512)S(1)} %copy-done.15), kind=kLoop, calls=%fused_computation.16 | loop fusion | flops 5240320 | bytes 5263360 | tf_op jit(solution)/shard_map/reduce_sum | solution.py:89
  74.9 0.3 copy-done.4
  75.2 0.7 multiply_convert_fusion.1
  75.9 0.5 copy-done.11
  76.4 1.7 fusion.45
  78.2 0.1 copy-done.22
  78.2 1.3 multiply_convert_fusion
  79.5 0.2 copy-done.8
  79.8 0.3 copy-done.20
  80.1 3.6 %fusion.6 = f32[1536,512]{1,0:T(8,128)} fusion(bf16[1024,512]{1,0:T(8,128)(2,1)S(1)} %multiply_convert_fusion, bf16[1024,512]{1,0:T(8,128)(2,1)S(1)} %copy-done.7, bf16[1024,512]{1,0:T(8,128)(2,1)S(1)} %copy-done.8, bf16[1024,512]{1,0:T(8,128)(2,1)S(1)} %bitcast.53), kind=kOutput, calls=%fused_computation.26 | convolution fusion | flops 1620049920 | bytes 7340032 | tf_op jit(solution)/shard_map/dot_general | solution.py:98
  83.7 4.5 %fusion.44 = f32[1024,1536]{1,0:T(8,128)} fusion(bf16[1024,512]{1,0:T(8,128)(2,1)S(1)} %multiply_convert_fusion, bf16[1536,512]{1,0:T(8,128)(2,1)S(1)} %copy-done), kind=kOutput, calls=%fused_computation.87 | convolution fusion | flops 1610612736 | bytes 8912896 | tf_op jit(solution)/shard_map/dot_general | solution.py:99
  88.1 8.4 %scatter_custom_fusion.1 = f32[576,512]{1,0:T(8,128)} fusion(s32[1024]{0:T(1024)S(1)} %copy-done.17, f32[1024,1536]{1,0:T(8,128)} %fusion.44, f32[]{:T(128)} %constant.10.clone.1), kind=kCustom, calls=%fused_computation.14 | custom fusion | flops 524288 | bytes 3277312 | tf_op jit(solution)/shard_map/scatter-add | solution.py:157
  96.6 1.3 convert.12
  98.0 3.1 %slice.64 = f32[1024,512]{1,0:T(8,128)} slice(f32[1024,1536]{1,0:T(8,128)} %fusion.44), slice={[0:1024], [0:512]} | slice | bytes 4194304 | tf_op jit(solution)/shard_map/slice | solution.py:100
  101.0 0.8 convert_element_type.83
  101.8 8.5 %all-to-all-start.1 = ((bf16[64,4,512]{2,1,0:T(4,128)(2,1)}), bf16[64,4,512]{2,1,0:T(4,128)(2,1)S(1)}, u32[]{:S(2)}, u32[]{:S(2)}) async-start(bf16[64,4,512]{2,1,0:T(4,128)(2,1)} %convert_element_type.83), calls=%async_computation.1 | async-start | bytes 524288 | tf_op jit(solution)/shard_map/all_to_all | solution.py:163
  110.3 1.7 collective-permute-start.2
  112.0 3.0 %copy.32 = f32[1024,512]{0,1:T(8,128)} copy(f32[1024,512]{1,0:T(8,128)} %slice.64) | data formatting | bytes 4194304
  114.9 142.1 %all-reduce.4 = (bf16[1536,512]{1,0:T(8,128)(2,1)}, bf16[512,512]{1,0:T(8,128)(2,1)}, bf16[1024,512]{1,0:T(8,128)(2,1)}, bf16[512,512]{1,0:T(8,128)(2,1)}, bf16[512]{0:T(512)(128)(2,1)}, /*index=5*/bf16[512]{0:T(512)(128)(2,1)}) all-reduce(f32[1536,512]{1,0:T(8,128)} %fusion.6, ...), channel_id=1, replica_groups=mesh['patch'=64,'sample'=4] {'patch','sample'}, use_global_device_ids=true, to_apply=%region_12.0 | all-reduce | flops 1836032 | bytes 11016192 | tf_op jit(solution)/shard_map/psum | solution.py:172
  257.0 2.9 %fusion.10 = bf16[1,1024,512]{1,2,0:T(8,128)(2,1)} fusion(f32[1024,512]{0,1:T(8,128)} %copy.32, bf16[1,1024,512]{1,2,0:T(8,128)(2,1)S(1)} %copy.25), kind=kLoop, calls=%fused_computation.31 | loop fusion | flops 1572864 | bytes 4194304 | tf_op jit(solution)/shard_map/broadcast_in_dim | solution.py:185
  259.9 2.4 copy.31
  262.3 1.2 fusion.21
  263.6 7.6 %scatter_custom_fusion.2 = f32[256,512]{1,0:T(8,128)S(1)} fusion(f32[256,512]{1,0:T(8,128)S(1)} %fusion.21, s32[1024]{0:T(1024)S(1)} %copy-done.18, f32[1024,1536]{1,0:T(8,128)} %fusion.44), kind=kCustom, calls=%fused_computation.12 | custom fusion | flops 524288 | bytes 2621440 | tf_op jit(solution)/shard_map/scatter-add | solution.py:105
  271.2 2.3 scatter_custom_fusion.3
  273.6 0.8 fusion.25
  (56 shorter events, 0.3 us)
Async XLA Ops:
  0.6 36.4 %copy-start = (bf16[1536,512]{1,0:T(8,128)(2,1)S(1)}, bf16[1536,512]{1,0:T(8,128)(2,1)}, u32[]{:S(2)}) copy-start(bf16[1536,512]{1,0:T(8,128)(2,1)} %param.20) | copy-start | bytes 4718596
  0.6 19.0 %copy-start.16 = (s32[64,4]{0,1:T(4,128)S(1)}, s32[64,4]{0,1:T(4,128)}, u32[]{:S(2)}) copy-start(s32[64,4]{0,1:T(4,128)} %param.19) | copy-start | bytes 3076
  0.7 17.2 %copy-start.1 = (bf16[1,256,512]{2,1,0:T(8,128)(2,1)S(1)}, bf16[1,256,512]{2,1,0:T(8,128)(2,1)}, u32[]{:S(2)}) copy-start(bf16[1,256,512]{2,1,0:T(8,128)(2,1)} %param.14) | copy-start | bytes 786436
  0.7 18.9 %copy-start.18 = (s32[1024]{0:T(1024)S(1)}, s32[1024]{0:T(1024)}, u32[]{:S(2)}) copy-start(s32[1024]{0:T(1024)} %param.18) | copy-start | bytes 12292
  0.7 18.9 %copy-start.17 = (s32[1024]{0:T(1024)S(1)}, s32[1024]{0:T(1024)}, u32[]{:S(2)}) copy-start(s32[1024]{0:T(1024)} %param.17) | copy-start | bytes 12292
  4.7 25.4 %all-to-all-start = ((bf16[64,4,512]{2,1,0:T(4,128)(2,1)}), bf16[64,4,512]{2,1,0:T(4,128)(2,1)S(1)}, u32[]{:S(2)}, u32[]{:S(2)}) async-start(bf16[64,4,512]{2,1,0:T(4,128)(2,1)} %reshape.83), calls=%async_computation | async-start | bytes 524288 | tf_op jit(solution)/shard_map/all_to_all | solution.py:141
  17.9 13.0 %collective-permute-start = (bf16[32,512]{1,0:T(8,128)(2,1)S(1)}, bf16[32,512]{1,0:T(8,128)(2,1)S(1)}, u32[]{:S(2)}, u32[]{:S(2)}) collective-permute-start(bf16[32,512]{1,0:T(8,128)(2,1)S(1)} %get-tuple-element.38), channel_id=1, source_target_pairs={{0,4},{4,8},{8,12},{12,16},{16,20},{20,24},{24,28},{28,32},{32,36}... | collective-permute-start | bytes 98312 | tf_op jit(solution)/shard_map/ppermute | solution.py:17
  19.6 11.3 %collective-permute-start.1 = (bf16[32,512]{1,0:T(8,128)(2,1)S(1)}, bf16[32,512]{1,0:T(8,128)(2,1)S(1)}, u32[]{:S(2)}, u32[]{:S(2)}) collective-permute-start(bf16[32,512]{1,0:T(8,128)(2,1)S(1)} %get-tuple-element.39), channel_id=1, source_target_pairs={{4,0},{8,4},{12,8},{16,12},{20,16},{24,20},{28,24},{32,28},{36,32}... | collective-permute-start | bytes 98312 | tf_op jit(solution)/shard_map/ppermute | solution.py:19
  37.0 5.3 %copy-start.13 = (bf16[512,512]{1,0:T(8,128)(2,1)S(1)}, bf16[512,512]{1,0:T(8,128)(2,1)}, u32[]{:S(2)}) copy-start(bf16[512,512]{1,0:T(8,128)(2,1)} %param.21) | copy-start | bytes 1572868
  42.2 1.1 copy-start.10
  42.2 2.1 copy-start.15
  43.0 1.3 copy-start.2
  56.4 1.8 copy-start.21
  58.2 1.0 copy-start.12
  58.2 0.9 copy-start.19
  60.0 1.6 copy-start.9
  62.0 1.8 copy-start.5
  71.7 3.2 %copy-start.3 = (f32[1024,512]{0,1:T(8,128)S(1)}, f32[1024,512]{0,1:T(8,128)}, u32[]{:S(2)}) copy-start(f32[1024,512]{0,1:T(8,128)} %copy-done.2) | copy-start | bytes 6291460
  71.7 3.5 %copy-start.4 = (f32[1024,512]{0,1:T(8,128)S(1)}, f32[1024,512]{0,1:T(8,128)}, u32[]{:S(2)}) copy-start(f32[1024,512]{0,1:T(8,128)} %copy.28) | copy-start | bytes 6291460
  75.2 1.2 copy-start.11
  76.4 1.7 copy-start.14
  76.4 1.8 copy-start.22
  78.2 1.3 copy-start.7
  78.2 1.5 copy-start.8
  78.2 1.9 copy-start.20
  101.8 169.4 %all-to-all-start.1 = ((bf16[64,4,512]{2,1,0:T(4,128)(2,1)}), bf16[64,4,512]{2,1,0:T(4,128)(2,1)S(1)}, u32[]{:S(2)}, u32[]{:S(2)}) async-start(bf16[64,4,512]{2,1,0:T(4,128)(2,1)} %convert_element_type.83), calls=%async_computation.1 | async-start | bytes 524288 | tf_op jit(solution)/shard_map/all_to_all | solution.py:163
  110.3 152.1 %collective-permute-start.2 = (bf16[32,512]{1,0:T(8,128)(2,1)S(1)}, bf16[32,512]{1,0:T(8,128)(2,1)S(1)}, u32[]{:S(2)}, u32[]{:S(2)}) collective-permute-start(bf16[32,512]{1,0:T(8,128)(2,1)S(1)} %get-tuple-element.36), channel_id=1, source_target_pairs={{0,4},{4,8},{8,12},{12,16},{16,20},{20,24},{24,28},{28,32},{32,36}... | collective-permute-start | bytes 98312 | tf_op jit(solution)/shard_map/ppermute | solution.py:28
  112.0 150.4 %collective-permute-start.3 = (bf16[32,512]{1,0:T(8,128)(2,1)S(1)}, bf16[32,512]{1,0:T(8,128)(2,1)S(1)}, u32[]{:S(2)}, u32[]{:S(2)}) collective-permute-start(bf16[32,512]{1,0:T(8,128)(2,1)S(1)} %get-tuple-element.37), channel_id=1, source_target_pairs={{0,252},{4,0},{8,4},{12,8},{16,12},{20,16},{24,20},{28,24},{32,28}... | collective-permute-start | bytes 98312 | tf_op jit(solution)/shard_map/ppermute | solution.py:28
  259.9 2.4 copy-start.6
where the time goes:
time: 277 us; the launch traced here: 274 us
  blocking collectives  142 us (51%)
  other arithmetic  40.4 us (15%)
  local copies, waits for them, and re-layouts  39.1 us (14%)
  starting transfers between devices  25 us (9%)
  matrix products  23.5 us (8%)
  waiting for transfers between devices  3.2 us (1%)
    psum x1, blocking collectives, on_device(): lax.psum((weight_terms[0], weight_terms[1], weight_terms[2], weight_terms...  142 us
    all_to_all x1, starting transfers between devices, on_device(): lax.all_to_all(outgoing, 'patch', split_axis=0, concat_axis=0, tiled=True)  13.2 us
    unnamed x50, local copies, waits for them, and re-layouts  9.64 us
    all_to_all x1, starting transfers between devices, on_device(): lax.all_to_all(far_grad.astype(jnp.bfloat16), 'patch', split_axis=0, conc...  8.46 us
    scatter-add x1, other arithmetic, on_device(): jax.ops.segment_sum(sent_grad, senders, num_segments=table.shape[0])  8.43 us
    gather x2, local copies, waits for them, and re-layouts, layer_backward(): node_input_grad[:, width:][recv_ids]  7.83 us
    scatter-add x1, other arithmetic, layer_backward(): jax.ops.segment_sum(edge_input_grad[:, 2 * width:], recv_ids, num_segment...  7.62 us
    scatter-add x1, other arithmetic, layer_backward(): jax.ops.segment_sum(update, recv_ids, num_segments=nodes_in.shape[0])  7.56 us
  transfers between devices with their start and end apart: 6, of which 1 were waited for; matrix products, arithmetic and copies ran while one was open for 9% of the time, Pallas kernels for 0%

commit v1 on v0

v1 whole, which is shorter than its diff:
```python
import functools

import jax
import jax.numpy as jnp
from jax import lax
from jax.experimental import pallas as pl
from jax.experimental.pallas import tpu as pltpu
from jax.sharding import PartitionSpec as P

RIM = 32
FAR = 4
MESH = pl.DeviceIdType.MESH
F32 = jnp.float32
BF16 = jnp.bfloat16
VMEM = pltpu.VMEM


def mm(a, b):
    return lax.dot_general(a, b, (((1,), (0,)), ((), ())), preferred_element_type=F32)


def mm_nt(a, b):
    return lax.dot_general(a, b, (((1,), (1,)), ((), ())), preferred_element_type=F32)


def mm_tn(a, b):
    return lax.dot_general(a, b, (((0,), (0,)), ((), ())), preferred_element_type=F32)


def one_hot_cols(col, width):
    parts = []
    lanes = lax.broadcasted_iota(jnp.int32, col.shape, 1)
    for start in range(0, width, 128):
        size = min(128, width - start)
        hit = (col == lanes + start).astype(F32).astype(BF16)
        parts.append(hit if size == 128 else hit[:, :size])
    return jnp.concatenate(parts, axis=1) if len(parts) > 1 else parts[0]


def one_hot_rows(row, height):
    ids = lax.broadcasted_iota(jnp.int32, (height, row.shape[1]), 0)
    return (ids == row).astype(F32).astype(BF16)


def normalize(values):
    center = values - jnp.mean(values, axis=1, keepdims=True)
    spread = jnp.mean(center * center, axis=1, keepdims=True)
    scale = lax.rsqrt(spread + 1e-05)
    return (center * scale, scale)


def normalize_back(grads, normed, scale):
    first = jnp.mean(grads, axis=1, keepdims=True)
    second = jnp.mean(grads * normed, axis=1, keepdims=True)
    return (grads - first - normed * second) * scale


def layer_kernel(
    lat, cot, nodes, ncot, low, high, far, senders, receivers,
    w1, w2, gain, nw1, nw2, ngain,
    edge_grad, node_partial, low_grad, high_grad, far_grad, terms, gains,
    onehot, projected, act, slope, hat, scale, raw_grad, pre_grad,
):
    edges, width = lat.shape
    count = nodes.shape[0]
    table = jnp.concatenate([low[...], nodes[...], high[...], far[...]], axis=0)
    rows = table.shape[0]
    block = 256
    projected[0:rows, :] = mm(table, w1[width : 2 * width, :]).astype(BF16)
    projected[rows : rows + count, :] = mm(nodes[...], w1[2 * width :, :]).astype(BF16)
    send_row = senders[...]
    recv_row = receivers[...]
    send_col = jnp.transpose(jnp.broadcast_to(send_row, (128, edges)))
    recv_col = jnp.transpose(jnp.broadcast_to(recv_row, (128, edges)))
    onehot[:, 0:rows] = one_hot_cols(send_col, rows)
    onehot[:, rows : rows + count] = one_hot_cols(recv_col, count)
    recv_rows = one_hot_rows(recv_row, count)
    edge_gain = gain[...]
    inflow = jnp.zeros((count, width), F32)
    for start in range(0, edges, block):
        part = slice(start, start + block)
        pre = mm(lat[part, :], w1[0:width, :]) + mm(onehot[part, :], projected[...])
        sig = jax.nn.sigmoid(pre)
        acted = (pre * sig).astype(BF16)
        act[part, :] = acted
        slope[part, :] = sig * (1.0 + pre * (1.0 - sig))
        normed, inv = normalize(mm(acted, w2[...]))
        hat[part, :] = normed
        scale[part, :] = inv
        inflow = inflow + mm(recv_rows[:, part], (normed * edge_gain).astype(BF16))
    inflow = inflow.astype(BF16)
    node_pre = mm(nodes[...], nw1[0:width, :]) + mm(inflow, nw1[width:, :])
    node_sig = jax.nn.sigmoid(node_pre)
    node_act = (node_pre * node_sig).astype(BF16)
    node_hat, node_scale = normalize(mm(node_act, nw2[...]))
    upstream = ncot[...].astype(F32)
    gains[1:2, :] = jnp.sum(upstream * node_hat, axis=0, keepdims=True)
    node_raw_grad = normalize_back(upstream * ngain[...], node_hat, node_scale).astype(BF16)
    node_act_grad = mm_nt(node_raw_grad, nw2[...])
    node_pre_grad = (node_act_grad * node_sig * (1.0 + node_pre * (1.0 - node_sig))).astype(BF16)

    def put(row, value):
        for j in range(width // 128):
            terms[j, row : row + value.shape[0], :] = value[:, 128 * j : 128 * j + 128].astype(BF16)

    put(4 * width, mm_tn(nodes[...], node_pre_grad))
    put(5 * width, mm_tn(inflow, node_pre_grad))
    put(6 * width, mm_tn(node_act, node_raw_grad))
    node_partial[...] = upstream + mm_nt(node_pre_grad, nw1[0:width, :])
    inflow_grad = mm_nt(node_pre_grad, nw1[width:, :]).astype(BF16)
    gain_grad = jnp.zeros((1, width), F32)
    for start in range(0, edges, block):
        part = slice(start, start + block)
        edge_cot = cot[part, :].astype(F32)
        normed = hat[part, :]
        update_grad = edge_cot + mm(onehot[part, rows : rows + count], inflow_grad)
        gain_grad = gain_grad + jnp.sum(update_grad * normed, axis=0, keepdims=True)
        back = normalize_back(update_grad * edge_gain, normed, scale[part, :]).astype(BF16)
        raw_grad[part, :] = back
        pre_back = (mm_nt(back, w2[...]) * slope[part, :]).astype(BF16)
        pre_grad[part, :] = pre_back
        edge_grad[part, :] = (edge_cot + mm_nt(pre_back, w1[0:width, :])).astype(BF16)
    gains[0:1, :] = gain_grad
    gains[2:8, :] = jnp.zeros((6, width), F32)
    all_pre = pre_grad[...]
    send_sum = mm(one_hot_rows(send_row, rows), all_pre).astype(BF16)
    recv_sum = mm(recv_rows, all_pre).astype(BF16)
    table_grad = mm_nt(send_sum, w1[width : 2 * width, :])
    low_grad[...] = table_grad[0:RIM, :].astype(BF16)
    high_grad[...] = table_grad[RIM + count : 2 * RIM + count, :].astype(BF16)
    far_grad[...] = table_grad[2 * RIM + count :, :].astype(BF16)
    node_partial[...] += table_grad[RIM : RIM + count, :] + mm_nt(recv_sum, w1[2 * width :, :])
    put(3 * width, mm_tn(act[...], raw_grad[...]))
    put(0, mm_tn(lat[...], all_pre))
    put(width, mm_tn(table, send_sum))
    put(2 * width, mm_tn(nodes[...], recv_sum))


def local_layer(lat, cot, nodes, ncot, low, high, far, senders, receivers, w1, w2, gain, nw1, nw2, ngain):
    edges, width = lat.shape
    count = nodes.shape[0]
    rows = count + 2 * RIM + far.shape[0]
    total = 7 * width
    shapes = (
        jax.ShapeDtypeStruct((edges, width), BF16),
        jax.ShapeDtypeStruct((count, width), F32),
        jax.ShapeDtypeStruct((RIM, width), BF16),
        jax.ShapeDtypeStruct((RIM, width), BF16),
        jax.ShapeDtypeStruct((far.shape[0], width), BF16),
        jax.ShapeDtypeStruct((width // 128, total, 128), BF16),
        jax.ShapeDtypeStruct((8, width), F32),
    )
    whole = pl.BlockSpec(memory_space=VMEM)
    return pl.pallas_call(
        layer_kernel,
        out_shape=shapes,
        in_specs=[whole] * 15,
        out_specs=(whole,) * 7,
        scratch_shapes=[
            VMEM((edges, rows + count), BF16),
            VMEM((rows + count, width), BF16),
            VMEM((edges, width), BF16),
            VMEM((edges, width), F32),
            VMEM((edges, width), F32),
            VMEM((edges, 1), F32),
            VMEM((edges, width), BF16),
            VMEM((edges, width), BF16),
        ],
        compiler_params=pltpu.CompilerParams(vmem_limit_bytes=48 * 1024 * 1024),
        cost_estimate=pl.CostEstimate(flops=8 * 10**9, bytes_accessed=20 * 10**6, transcendentals=10**6),
        name="local_layer",
    )(
        lat, cot, nodes, ncot, low, high, far, senders.reshape(1, edges), receivers.reshape(1, edges),
        w1, w2, gain.reshape(1, width), nw1, nw2, ngain.reshape(1, width),
    )


def with_halo_parts(cells, axis, width):
    count = lax.axis_size(axis)
    low = lax.ppermute(cells[cells.shape[0] - width :], axis, [(i, (i + 1) % count) for i in range(count)])
    high = lax.ppermute(cells[:width], axis, [((i + 1) % count, i) for i in range(count)])
    return low, high


def from_behind(array, axis, by):
    size = lax.axis_size(axis)
    return lax.ppermute(array, axis, [(i, (i + by) % size) for i in range(size)])


def on_device(
    edge_latents, node_latents, edge_cotangent, node_cotangent, senders, receivers, send_rows,
    edge_first, edge_second, edge_gain, node_first, node_second, node_gain,
):
    patches = lax.axis_size("patch")
    own = node_latents[0]
    count, width = own.shape
    outgoing = own[send_rows]
    far = lax.all_to_all(outgoing, "patch", split_axis=0, concat_axis=0, tiled=True).reshape(patches * FAR, width)
    low, high = with_halo_parts(own, "patch", RIM)
    edge_grad, node_partial, low_grad, high_grad, far_grad, terms, gains = local_layer(
        edge_latents[0], edge_cotangent[0], own, node_cotangent[0], low, high, far, senders, receivers,
        edge_first, edge_second, edge_gain, node_first, node_second, node_gain,
    )
    from_next = from_behind(low_grad, "patch", -1).astype(F32)
    from_prev = from_behind(high_grad, "patch", 1).astype(F32)
    returned = lax.all_to_all(
        far_grad.reshape(patches, FAR, width), "patch", split_axis=0, concat_axis=0, tiled=True
    ).astype(F32)
    node_total = node_partial + jnp.pad(from_prev, ((0, count - RIM), (0, 0)))
    node_total = node_total + jnp.pad(from_next, ((count - RIM, 0), (0, 0)))
    node_total = node_total + jax.ops.segment_sum(
        returned.reshape(patches * FAR, width), send_rows.reshape(-1), num_segments=count
    )
    summed, gains = lax.psum((terms.astype(F32), gains), ("patch", "sample"))
    summed = summed.astype(BF16)
    flat = jnp.concatenate([summed[j] for j in range(4)], axis=1)
    return (
        edge_grad[None],
        node_total.astype(BF16)[None],
        flat[: 3 * width],
        flat[3 * width : 4 * width],
        flat[4 * width : 6 * width],
        flat[6 * width :],
        gains[0].astype(BF16),
        gains[1].astype(BF16),
    )


def solution(mesh):
    return jax.shard_map(
        on_device,
        mesh=mesh,
        in_specs=(
            P("sample", "patch", None), P("sample", "patch", None), P("sample", "patch", None),
            P("sample", "patch", None), P("patch"), P("patch"), P("patch", None),
            P(), P(), P(), P(), P(), P(),
        ),
        out_specs=(P("sample", "patch", None), P("sample", "patch", None), P(), P(), P(), P(), P(), P()),
        check_vma=False,
    )
```

time: 277 us -> 338 us (1.22)
  waiting for transfers between devices: 3.2 us -> 179 us
  blocking collectives: 142 us -> 81.8 us
  other arithmetic: 40.4 us -> 6.55 us
  matrix products: 23.5 us -> 0 us
  local copies, waits for them, and re-layouts: 39.1 us -> 16.1 us
  Pallas kernels: 0 us -> 15.9 us
  between operations: 1.03 us -> 14.2 us
    psum x0 -> x1, waiting for transfers between devices: none -> 170 us  [on_device(): summed, gains = lax.psum((terms.astype(F32), gains), ('patch', 'sample'))]
    psum x1, blocking collectives: 142 us -> 81.8 us  [on_device(): summed, gains = lax.psum((terms.astype(F32), gains), ('patch', 'sample'))]
    scatter-add x3 -> x0, other arithmetic: 23.6 us -> none  [the longest x1 8.43 us: on_device(): jax.ops.segment_sum(sent_grad, senders, num_segments=table.shape[0])]
    dot_general x12 -> x0, matrix products: 23.5 us -> none  [the longest x1 5.26 us: layer_backward(): jnp.dot(edge_input, edge_first, preferred_element_type=jnp.float32)]
    gather x6 -> x2, local copies, waits for them, and re-layouts: 21 us -> 2.96 us  [on_device(): outgoing = own[send_rows]]
    pallas_call x0 -> x1, Pallas kernels: none -> 15.9 us  [local_layer(): pl.pallas_call(layer_kernel, out_shape=shapes, in_specs=[whole] * 15, out...]
    all_to_all x1, waiting for transfers between devices: 3.18 us -> 9.81 us  [on_device(): lax.all_to_all(outgoing, 'patch', split_axis=0, concat_axis=0, tiled=True)]
    reduce_sum x4 -> x0, other arithmetic: 4.03 us -> none  [the longest x1 3.2 us: layer_backward(): edge_gain_grad = jnp.sum(update_grad * edge_hat, axis=0)]
  transfers between devices with their start and end apart: 6 -> 7, of which waited for: 1 -> 2; matrix products, arithmetic and copies ran while one was open for 9% -> 2% of each run, Pallas kernels for 0% -> 0%
where the time goes in v1:
time: 338 us; the launch traced here: 337 us
  waiting for transfers between devices  179 us (53%)
  blocking collectives  81.8 us (24%)
  starting transfers between devices  22.6 us (7%)
  local copies, waits for them, and re-layouts  16.1 us (5%)
  Pallas kernels  15.9 us (5%)
  between operations  14.2 us (4%)
  other arithmetic  6.55 us (2%)
    psum x1, waiting for transfers between devices, on_device(): summed, gains = lax.psum((terms.astype(F32), gains), ('patch', 'sample'))  170 us
    psum x1, blocking collectives, on_device(): summed, gains = lax.psum((terms.astype(F32), gains), ('patch', 'sample'))  81.8 us
    pallas_call x1, Pallas kernels, local_layer(): pl.pallas_call(layer_kernel, out_shape=shapes, in_specs=[whole] * 15, out...  15.9 us
    all_to_all x1, starting transfers between devices, on_device(): lax.all_to_all(outgoing, 'patch', split_axis=0, concat_axis=0, tiled=True)  13.2 us
    all_to_all x1, waiting for transfers between devices, on_device(): lax.all_to_all(outgoing, 'patch', split_axis=0, concat_axis=0, tiled=True)  9.81 us
    unnamed x25, local copies, waits for them, and re-layouts  7.1 us
  transfers between devices with their start and end apart: 7, of which 2 were waited for; matrix products, arithmetic and copies ran while one was open for 2% of the time, Pallas kernels for 0%

profile of v1, /device:TPU:1, one launch (start us, length us, event | category | flops | bytes accessed | tf_op | source)
XLA Modules:
  0.0 336.7 jit_solution(7254957327424648653)
XLA Ops:
  7.2 0.0 copy-start
  7.2 0.0 copy-start.1
  7.2 0.0 copy-start.2
  7.2 0.8 compare_select_fusion
  8.0 0.1 copy.21
  8.1 0.1 reshape.56
  8.3 2.2 gather_fusion
  10.5 0.8 reshape.55
  11.2 13.2 %all-to-all-start = ((bf16[64,4,512]{2,1,0:T(4,128)(2,1)}), bf16[64,4,512]{2,1,0:T(4,128)(2,1)S(1)}, u32[]{:S(2)}, u32[]{:S(2)}) async-start(bf16[64,4,512]{2,1,0:T(4,128)(2,1)} %reshape.55), calls=%async_computation | async-start | bytes 524288 | tf_op jit(solution)/shard_map/all_to_all | solution.py:198
  24.4 0.0 all-reduce.4.cloned.1.call-start
  24.4 0.8 slice_bitcast_fusion.4
  25.2 1.6 collective-permute-start
  26.9 0.0 collective-permute-start.1
  26.9 9.8 %all-to-all-done = bf16[64,4,512]{2,1,0:T(4,128)(2,1)S(1)} async-done(((bf16[64,4,512]{2,1,0:T(4,128)(2,1)}), bf16[64,4,512]{2,1,0:T(4,128)(2,1)S(1)}, u32[]{:S(2)}, u32[]{:S(2)}) %all-to-all-start) | async-done | bytes 262176 | tf_op jit(solution)/shard_map/all_to_all | solution.py:198
  36.7 0.1 reshape.44.far
  36.7 0.0 collective-permute-done.low
  36.7 0.0 collective-permute-done.1.high
  36.8 0.0 copy-done
  36.8 0.0 copy-done.1
  36.8 0.0 copy-done.2
  36.8 0.0 copy-start.3
  36.8 1.2 copy-done.3
  38.0 0.0 copy-start.4
  38.0 1.0 copy-done.4
  39.1 0.0 copy-start.5
  39.1 1.0 copy-done.5
  40.1 0.0 copy-start.6
  40.1 0.9 copy-done.6
  41.1 0.0 copy-start.7
  41.1 0.7 copy-done.7
  41.7 0.0 copy-start.8
  41.7 0.7 copy-done.8
  42.4 0.0 copy-start.9
  42.4 0.7 copy-done.9
  43.1 0.0 copy-start.10
  43.1 0.7 copy-done.10
  43.8 15.9 %local_layer.1 = (bf16[1024,512]{1,0:T(8,128)(2,1)}, f32[256,512]{1,0:T(8,128)S(1)}, bf16[32,512]{1,0:T(8,128)(2,1)S(1)}, bf16[32,512]{1,0:T(8,128)(2,1)S(1)}, b...) custom-call(bf16[1024,512]{1,0:T(8,128)(2,1)S(1)} %bitcast.25, ...), custom_call_target="tpu_custom_call" | custom-call | flops 8000000000 | bytes 20000000 | tf_op jit(solution)/shard_map/local_layer/pallas_call | solution.py:154
  59.7 0.0 copy-start.11
  59.7 0.0 all-reduce.4.cloned.1.call-update
  59.7 0.8 reshape.49
  60.5 5.8 %all-to-all-start.1 = ((bf16[64,4,512]{2,1,0:T(4,128)(2,1)}), bf16[64,4,512]{2,1,0:T(4,128)(2,1)S(1)}, u32[]{:S(2)}, u32[]{:S(2)}) async-start(bf16[64,4,512]{2,1,0:T(4,128)(2,1)} %reshape.49), calls=%async_computation.1 | async-start | bytes 524288 | tf_op jit(solution)/shard_map/all_to_all | solution.py:206
  66.3 0.0 copy-done.11
  66.3 0.1 copy.22
  66.4 0.1 reshape.64
  66.5 0.5 collective-permute-start.3
  67.0 1.5 collective-permute-start.2
  68.5 81.8 %psum.15 = bf16[8,512]{1,0:T(8,128)(2,1)S(1)} all-reduce(f32[8,512]{1,0:T(8,128)S(1)} %get-tuple-element.21), channel_id=1, replica_groups=mesh['patch'=64,'sample'=4] {'patch','sample'}, use_global_device_ids=true, to_apply=%region_2.3 | all-reduce | flops 4096 | bytes 24576 | tf_op jit(solution)/shard_map/psum | solution.py:214
  150.4 0.6 slice_reduce_fusion
  150.9 0.0 collective-permute-done.3
  150.9 0.0 collective-permute-done.2
  151.0 0.0 all-to-all-done.1
  151.0 2.3 scatter_fusion
  153.4 0.7 convert_bitcast_fusion
  154.1 169.6 %all-reduce.4.cloned.1.call-done = bf16[4,3584,128]{2,1,0:T(8,128)(2,1)} async-done(((bf16[4,3584,128]{2,1,0:T(8,128)(2,1)}), bf16[4,3584,128]{2,1,0:T(8,128)(2,1)}) %all-reduce.4.cloned.1.call-update) | async-done | bytes 3670032 | tf_op jit(solution)/shard_map/psum | solution.py:214
  323.7 2.3 slice_bitcast_fusion.3
  326.0 0.4 pad_maximum_fusion
  326.5 1.1 pad_maximum_fusion.2
  327.6 1.1 pad_maximum_fusion.1
  328.7 1.2 slice.64
  (3 shorter events, 0.1 us)
Async XLA Ops:
  7.2 29.6 %copy-start = (bf16[1,256,512]{2,1,0:T(8,128)(2,1)S(1)}, bf16[1,256,512]{2,1,0:T(8,128)(2,1)}, u32[]{:S(2)}) copy-start(bf16[1,256,512]{2,1,0:T(8,128)(2,1)} %param.14) | copy-start | bytes 786436
  7.2 29.6 %copy-start.1 = (bf16[1,1024,512]{2,1,0:T(8,128)(2,1)S(1)}, bf16[1,1024,512]{2,1,0:T(8,128)(2,1)}, u32[]{:S(2)}) copy-start(bf16[1,1024,512]{2,1,0:T(8,128)(2,1)} %param.13) | copy-start | bytes 3145732
  7.2 29.6 %copy-start.2 = (bf16[1,1024,512]{2,1,0:T(8,128)(2,1)S(1)}, bf16[1,1024,512]{2,1,0:T(8,128)(2,1)}, u32[]{:S(2)}) copy-start(bf16[1,1024,512]{2,1,0:T(8,128)(2,1)} %param.15) | copy-start | bytes 3145732
  11.2 25.4 %all-to-all-start = ((bf16[64,4,512]{2,1,0:T(4,128)(2,1)}), bf16[64,4,512]{2,1,0:T(4,128)(2,1)S(1)}, u32[]{:S(2)}, u32[]{:S(2)}) async-start(bf16[64,4,512]{2,1,0:T(4,128)(2,1)} %reshape.55), calls=%async_computation | async-start | bytes 524288 | tf_op jit(solution)/shard_map/all_to_all | solution.py:198
  24.4 299.4 %all-reduce.4.cloned.1.call-start = ((), (), s32[]{:S(2)}) async-start(), calls=%async_computation.2 | async-start | bytes 7340032 | tf_op jit(solution)/shard_map/psum | solution.py:214
  25.2 11.5 %collective-permute-start = (bf16[32,512]{1,0:T(8,128)(2,1)S(1)}, bf16[32,512]{1,0:T(8,128)(2,1)S(1)}, u32[]{:S(2)}, u32[]{:S(2)}) collective-permute-start(bf16[32,512]{1,0:T(8,128)(2,1)S(1)} %get-tuple-element.31), channel_id=1, source_target_pairs={{0,4},{4,8},{8,12},{12,16},{16,20},{20,24},{24,28},{28,32},{32,36}... | collective-permute-start | bytes 98312 | tf_op jit(solution)/shard_map/ppermute | solution.py:180
  26.9 9.9 %collective-permute-start.1 = (bf16[32,512]{1,0:T(8,128)(2,1)S(1)}, bf16[32,512]{1,0:T(8,128)(2,1)S(1)}, u32[]{:S(2)}, u32[]{:S(2)}) collective-permute-start(bf16[32,512]{1,0:T(8,128)(2,1)S(1)} %get-tuple-element.30), channel_id=1, source_target_pairs={{4,0},{8,4},{12,8},{16,12},{20,16},{24,20},{28,24},{32,28},{36,32}... | collective-permute-start | bytes 98312 | tf_op jit(solution)/shard_map/ppermute | solution.py:181
  36.8 1.2 copy-start.3
  38.0 1.0 copy-start.4
  39.1 1.0 copy-start.5
  40.1 0.9 copy-start.6
  41.1 0.7 copy-start.7
  41.7 0.7 copy-start.8
  42.4 0.7 copy-start.9
  43.1 0.7 copy-start.10
  59.7 6.6 %copy-start.11 = (s32[64,4]{0,1:T(4,128)S(1)}, s32[64,4]{0,1:T(4,128)}, u32[]{:S(2)}) copy-start(s32[64,4]{0,1:T(4,128)} %param.19) | copy-start | bytes 3076
  60.5 90.5 %all-to-all-start.1 = ((bf16[64,4,512]{2,1,0:T(4,128)(2,1)}), bf16[64,4,512]{2,1,0:T(4,128)(2,1)S(1)}, u32[]{:S(2)}, u32[]{:S(2)}) async-start(bf16[64,4,512]{2,1,0:T(4,128)(2,1)} %reshape.49), calls=%async_computation.1 | async-start | bytes 524288 | tf_op jit(solution)/shard_map/all_to_all | solution.py:206
  66.5 84.5 %collective-permute-start.3 = (bf16[32,512]{1,0:T(8,128)(2,1)S(1)}, bf16[32,512]{1,0:T(8,128)(2,1)S(1)}, u32[]{:S(2)}, u32[]{:S(2)}) collective-permute-start(bf16[32,512]{1,0:T(8,128)(2,1)S(1)} %get-tuple-element.18), channel_id=1, source_target_pairs={{0,252},{4,0},{8,4},{12,8},{16,12},{20,16},{24,20},{28,24},{32,28}... | collective-permute-start | bytes 98312 | tf_op jit(solution)/shard_map/ppermute | solution.py:187
  67.0 83.9 %collective-permute-start.2 = (bf16[32,512]{1,0:T(8,128)(2,1)S(1)}, bf16[32,512]{1,0:T(8,128)(2,1)S(1)}, u32[]{:S(2)}, u32[]{:S(2)}) collective-permute-start(bf16[32,512]{1,0:T(8,128)(2,1)S(1)} %get-tuple-element.17), channel_id=1, source_target_pairs={{0,4},{4,8},{8,12},{12,16},{16,20},{20,24},{24,28},{28,32},{32,36}... | collective-permute-start | bytes 98312 | tf_op jit(solution)/shard_map/ppermute | solution.py:187
Sparse Core Ops, SparseCore 0:
  59.9 263.8 all-reduce.3

commit v2 on v1

--- a/solution.py
+++ b/solution.py
@@ -40,6 +40,26 @@
 def one_hot_rows(row, height):
     ids = lax.broadcasted_iota(jnp.int32, (height, row.shape[1]), 0)
     return (ids == row).astype(F32).astype(BF16)
+
+
+def spread_far(c, rows, by_patch):
+    at = lax.broadcasted_iota(jnp.int32, (4 * rows, rows), 0)
+    col = lax.broadcasted_iota(jnp.int32, (4 * rows, rows), 1)
+    patch, r = at // 16, at % 4
+    target = patch * FAR + r if by_patch else r * (rows // FAR) + patch
+    return ((col == target) & ((at // 4) % 4 == c)).astype(F32).astype(BF16)
+
+
+def gather_far(c, rows, by_patch):
+    at = lax.broadcasted_iota(jnp.int32, (rows, 4 * rows), 1)
+    row = lax.broadcasted_iota(jnp.int32, (rows, 4 * rows), 0)
+    patch, r = at // 16, at % 4
+    target = patch * FAR + r if by_patch else r * (rows // FAR) + patch
+    return ((row == target) & ((at // 4) % 4 == c)).astype(F32).astype(BF16)
+
+
+def send_one_hot(send_rows, count):
+    return jnp.concatenate([one_hot_rows(send_rows[r : r + 1, :], count) for r in range(FAR)], axis=1)
 
 
 def normalize(values):
@@ -94,7 +114,7 @@
     node_act = (node_pre * node_sig).astype(BF16)
     node_hat, node_scale = normalize(mm(node_act, nw2[...]))
     upstream = ncot[...].astype(F32)
-    gains[1:2, :] = jnp.sum(upstream * node_hat, axis=0, keepdims=True)
+    node_gain_grad = jnp.sum(upstream * node_hat, axis=0, keepdims=True)
     node_raw_grad = normalize_back(upstream * ngain[...], node_hat, node_scale).astype(BF16)
     node_act_grad = mm_nt(node_raw_grad, nw2[...])
     node_pre_grad = (node_act_grad * node_sig * (1.0 + node_pre * (1.0 - node_sig))).astype(BF16)
@@ -120,15 +140,20 @@
         pre_back = (mm_nt(back, w2[...]) * slope[part, :]).astype(BF16)
         pre_grad[part, :] = pre_back
         edge_grad[part, :] = (edge_cot + mm_nt(pre_back, w1[0:width, :])).astype(BF16)
-    gains[0:1, :] = gain_grad
-    gains[2:8, :] = jnp.zeros((6, width), F32)
+    for j in range(width // 128):
+        gains[j : j + 1, :] = gain_grad[:, 128 * j : 128 * j + 128]
+        gains[4 + j : 5 + j, :] = node_gain_grad[:, 128 * j : 128 * j + 128]
     all_pre = pre_grad[...]
     send_sum = mm(one_hot_rows(send_row, rows), all_pre).astype(BF16)
     recv_sum = mm(recv_rows, all_pre).astype(BF16)
     table_grad = mm_nt(send_sum, w1[width : 2 * width, :])
     low_grad[...] = table_grad[0:RIM, :].astype(BF16)
     high_grad[...] = table_grad[RIM + count : 2 * RIM + count, :].astype(BF16)
-    far_grad[...] = table_grad[2 * RIM + count :, :].astype(BF16)
+    far_rows = table_grad[2 * RIM + count :, :].astype(BF16)
+    packed = jnp.zeros((4 * far_rows.shape[0], 128), F32)
+    for c in range(width // 128):
+        packed = packed + mm(spread_far(c, far_rows.shape[0], True), far_rows[:, 128 * c : 128 * c + 128])
+    far_grad[...] = packed.astype(BF16)
     node_partial[...] += table_grad[RIM : RIM + count, :] + mm_nt(recv_sum, w1[2 * width :, :])
     put(3 * width, mm_tn(act[...], raw_grad[...]))
     put(0, mm_tn(lat[...], all_pre))
@@ -146,9 +171,9 @@
         jax.ShapeDtypeStruct((count, width), F32),
         jax.ShapeDtypeStruct((RIM, width), BF16),
         jax.ShapeDtypeStruct((RIM, width), BF16),
-        jax.ShapeDtypeStruct((far.shape[0], width), BF16),
+        jax.ShapeDtypeStruct((4 * far.shape[0], 128), BF16),
         jax.ShapeDtypeStruct((width // 128, total, 128), BF16),
-        jax.ShapeDtypeStruct((8, width), F32),
+        jax.ShapeDtypeStruct((8, 128), F32),
     )
     whole = pl.BlockSpec(memory_space=VMEM)
     return pl.pallas_call(
@@ -175,54 +200,420 @@
     )
 
 
-def with_halo_parts(cells, axis, width):
-    count = lax.axis_size(axis)
-    low = lax.ppermute(cells[cells.shape[0] - width :], axis, [(i, (i + 1) % count) for i in range(count)])
-    high = lax.ppermute(cells[:width], axis, [((i + 1) % count, i) for i in range(count)])
-    return low, high
-
-
-def from_behind(array, axis, by):
-    size = lax.axis_size(axis)
-    return lax.ppermute(array, axis, [(i, (i + by) % size) for i in range(size)])
+def place():
+    here = lax.axis_index("patch")
+    return here, lax.axis_index("sample"), lax.div(here, 16), lax.rem(lax.div(here, 2), 8), lax.rem(here, 2)
+
+
+def ring(here, count, step):
+    return lax.rem(here + (step + count) % count, count)
+
+
+def signal(patch, sample):
+    pl.semaphore_signal(
+        pltpu.get_barrier_semaphore(), inc=1, device_id={"patch": patch, "sample": sample}, device_id_type=MESH
+    )
+
+
+def send(src, dst, send_sem, recv_sem, patch, sample):
+    copy = pltpu.make_async_remote_copy(
+        src_ref=src, dst_ref=dst, send_sem=send_sem, recv_sem=recv_sem,
+        device_id={"patch": patch, "sample": sample}, device_id_type=MESH,
+    )
+    copy.start()
+    return copy
+
+
+def await_bytes(ref, sem):
+    pltpu.make_async_copy(ref, ref, sem).wait()
+
+
+def rows_at(start, size, align=16):
+    return pl.ds(pl.multiple_of(start, align), size)
+
+
+def exchange_kernel(nodes, send_rows, low, high, far, out, incoming, far_send, far_recv, rim_send, rim_recv):
+    here, sample, _, _, _ = place()
+    patches = send_rows.shape[1]
+    count, width = nodes.shape
+    behind, ahead = ring(here, patches, -1), ring(here, patches, 1)
+
+    def greet(k, carry):
+        signal(lax.rem(here + k, patches), sample)
+        return carry
+
+    lax.fori_loop(1, patches, greet, 0)
+    chosen = mm_tn(send_one_hot(send_rows[...], count), nodes[...]).astype(BF16)
+    packed = jnp.zeros(out.shape, F32)
+    for c in range(width // 128):
+        packed = packed + mm(spread_far(c, FAR * patches, False), chosen[:, 128 * c : 128 * c + 128])
+    out[...] = packed.astype(BF16)
+    pl.semaphore_wait(pltpu.get_barrier_semaphore(), patches - 1)
+    rims = (
+        send(nodes.at[count - RIM : count], low, rim_send.at[0], rim_recv.at[0], ahead, sample),
+        send(nodes.at[0:RIM], high, rim_send.at[1], rim_recv.at[1], behind, sample),
+    )
+
+    def push(k, carry):
+        to = lax.rem(here + k, patches)
+        send(out.at[rows_at(to * 16, 16)], incoming.at[rows_at(here * 16, 16)], far_send, far_recv, to, sample)
+        return carry
+
+    lax.fori_loop(1, patches, push, 0)
+    mine = rows_at(here * 16, 16)
+    incoming[mine, :] = out[mine, :]
+    await_bytes(incoming.at[0 : 16 * (patches - 1)], far_recv)
+    for c in range(width // 128):
+        far[:, 128 * c : 128 * c + 128] = mm(gather_far(c, FAR * patches, True), incoming[...]).astype(BF16)
+    await_bytes(out.at[0 : 16 * (patches - 1)], far_send)
+    for copy in rims:
+        copy.wait()
+
+
+def exchange(nodes, send_rows):
+    count, width = nodes.shape
+    patches = send_rows.shape[1]
+    whole = pl.BlockSpec(memory_space=VMEM)
+    return pl.pallas_call(
+        exchange_kernel,
+        out_shape=(
+            jax.ShapeDtypeStruct((RIM, width), BF16),
+            jax.ShapeDtypeStruct((RIM, width), BF16),
+            jax.ShapeDtypeStruct((FAR * patches, width), BF16),
+        ),
+        in_specs=[whole] * 2,
+        out_specs=(whole,) * 3,
+        scratch_shapes=[
+            VMEM((16 * patches, 128), BF16),
+            VMEM((16 * patches, 128), BF16),
+            pltpu.SemaphoreType.DMA,
+            pltpu.SemaphoreType.DMA,
+            pltpu.SemaphoreType.DMA((2,)),
+            pltpu.SemaphoreType.DMA((2,)),
+        ],
+        compiler_params=pltpu.CompilerParams(
+            collective_id=0, has_side_effects=True, vmem_limit_bytes=16 * 1024 * 1024
+        ),
+        name="exchange",
+    )(nodes, send_rows)
+
+
+def reduce_kernel(
+    terms, gains, far_grad, low_grad, high_grad, node_partial, send_rows,
+    total, gain_total, node_grad,
+    core_in, summed, first_in, second_in, second, z_out, z_in, z_done, returned, from_prev, from_next, gain_in,
+    core_sems, first_sems, second_sems, z_sems, back_sems, rim_sems, gather2_sems, gather1_sems, last_sems, gain_sems,
+):
+    here, x, y, z, core = place()
+    patches = send_rows.shape[1]
+    half = terms.shape[1] // 2
+    large, small = half // 4, half // 16
+    sibling = here + 1 - 2 * core
+    xs = [(x, here)] + [(ring(x, 4, s), here) for s in (1, 2, 3)]
+    ys = [(x, here)] + [(x, ring(y, 4, s) * 16 + z * 2 + core) for s in (1, 2, 3)]
+    axes = ((x, xs), (y, ys))
+    behind, ahead = ring(here, patches, -1), ring(here, patches, 1)
+
+    def greet(k, carry):
+        signal(lax.rem(here + k, patches), x)
+        return carry
+
+    for s in (1, 2, 3):
+        signal(here, ring(x, 4, s))
+    lax.fori_loop(1, patches, greet, 0)
+    pl.semaphore_wait(pltpu.get_barrier_semaphore(), patches + 2)
+
+    pending = []
+
+    def post(src, dst, sems, index, device):
+        copy = send(src, dst, sems.at[(0,) + index], sems.at[(1,) + index], device[1], device[0])
+        pending.append(copy)
+        return copy
+
+    def pair(h):
+        return slice(2 * h, 2 * h + 2)
+
+    order = (2, 1, 3, 0)
+    cores = {}
+    for k, s in enumerate(order):
+        for h in (0, 1):
+            at = ring(axes[h][0], 4, s) * large
+            cores[h, s] = post(
+                terms.at[pair(h), rows_at((1 - core) * half + at, large)],
+                core_in.at[pair(h), rows_at(at, large)], core_sems, (h, k), (x, sibling),
+            )
+    gain_copy = post(gains, gain_in.at[0], gain_sems, (0,), (x, sibling))
+    rims = (
+        post(high_grad, from_prev, rim_sems, (0,), (x, ahead)),
+        post(low_grad, from_next, rim_sems, (1,), (x, behind)),
+    )
+
+    def push(k, carry):
+        to = lax.rem(here + k, patches)
+        send(
+            far_grad.at[rows_at(to * 16, 16)], returned.at[rows_at(here * 16, 16)],
+            back_sems.at[0], back_sems.at[1], to, x,
+        )
+        return carry
+
+    def scatter(rows, size, device, pos, ready, take, source, landing, sems, h):
+        copies = {}
+        a, b = 2 * h, 2 * h + 1
+
+        def chunk(s):
+            return rows_at(rows(ring(pos, 4, s)), size)
+
+        def go(index, j, s, to):
+            copies[index] = post(source.at[j, chunk(s)], landing.at[h, index], sems, (h, index), device[to])
+
+        ready(h, 2)
+        go(0, a, 2, 1)
+        go(1, b, 2, 3)
+        ready(h, 1)
+        go(2, b, 1, 1)
+        ready(h, 3)
+        go(3, a, 3, 3)
+        return copies, chunk, go
+
+    def relay(state, h, source, landing):
+        copies, chunk, go = state
+        a, b = 2 * h, 2 * h + 1
+        copies[0].wait_recv()
+        source[a, chunk(1)] = (source[a, chunk(1)].astype(F32) + landing[h, 0].astype(F32)).astype(BF16)
+        go(4, a, 1, 1)
+        copies[1].wait_recv()
+        source[b, chunk(3)] = (source[b, chunk(3)].astype(F32) + landing[h, 1].astype(F32)).astype(BF16)
+        go(5, b, 3, 3)
+
+    def finish(state, h, source, landing):
+        copies, chunk, _ = state
+        a, b = 2 * h, 2 * h + 1
+        copies[3].wait_recv()
+        copies[4].wait_recv()
+        first = source[a, chunk(0)].astype(F32) + landing[h, 3].astype(F32) + landing[h, 4].astype(F32)
+        copies[2].wait_recv()
+        copies[5].wait_recv()
+        other = source[b, chunk(0)].astype(F32) + landing[h, 2].astype(F32) + landing[h, 5].astype(F32)
+        return first, other
+
+    def core_ready(h, s):
+        cores[h, s].wait_recv()
+        at = ring(axes[h][0], 4, s) * large
+        for j in (2 * h, 2 * h + 1):
+            mine = terms[j, rows_at(core * half + at, large)].astype(F32)
+            summed[j, rows_at(at, large)] = (mine + core_in[j, rows_at(at, large)].astype(F32)).astype(BF16)
+
+    states = [
+        scatter(lambda q: q * large, large, axes[h][1], axes[h][0], core_ready, None, summed, first_in, first_sems, h)
+        for h in (0, 1)
+    ]
+    lax.fori_loop(1, patches, push, 0)
+    for h in (0, 1):
+        core_ready(h, 0)
+    gain_copy.wait_recv()
+    gain_sum = jnp.where(core == 0, gains[...] + gain_in[0], gain_in[0] + gains[...])
+
+    def share_gain(value, base, count, pos, devices, index):
+        gain_in[base + pos] = value
+        for s in range(1, count):
+            send(
+                gain_in.at[base + pos], gain_in.at[base + pos], gain_sems.at[0, index], gain_sems.at[1, index],
+                devices[s][1], devices[s][0],
+            )
+
+    def gain_done(base, count, index):
+        await_bytes(gain_in.at[base : base + count - 1], gain_sems.at[1, index])
+        await_bytes(gain_in.at[base : base + count - 1], gain_sems.at[0, index])
+        result = gain_in[base]
+        for s in range(1, count):
+            result = result + gain_in[base + s]
+        return result
+
+    share_gain(gain_sum, 1, 4, x, xs, 1)
+    for h in (0, 1):
+        relay(states[h], h, summed, first_in)
+    for h in (0, 1):
+        first, other = finish(states[h], h, summed, first_in)
+        second[2 * h] = first.astype(BF16)
+        second[2 * h + 1] = other.astype(BF16)
+    swapped = (axes[1], axes[0])
+    states = [
+        scatter(
+            lambda q: q * small, small, swapped[h][1], swapped[h][0], lambda h, s: None, None,
+            second, second_in, second_sems, h,
+        )
+        for h in (0, 1)
+    ]
+    share_gain(gain_done(1, 4, 1), 5, 4, y, ys, 2)
+    for h in (0, 1):
+        relay(states[h], h, second, second_in)
+    piece = small // 2
+    z_out[...] = jnp.zeros(z_out.shape, BF16)
+    for h in (0, 1):
+        for j, value in enumerate(finish(states[h], h, second, second_in)):
+            for k in (0, 1):
+                z_out[(2 * h + j) * 2 + k, 0:piece, :] = value[piece * k : piece * (k + 1), :].astype(BF16)
+    zs = [(x, here)] + [(x, y * 16 + ring(z, 8, s) * 2 + core) for s in range(1, 8)]
+    for s in range(1, 8):
+        send(z_out.at[ring(z, 8, s)], z_in.at[z], z_sems.at[0, 0], z_sems.at[1, 0], zs[s][1], zs[s][0])
+    z_in[z] = z_out[z]
+    share_gain(gain_done(5, 4, 2), 9, 8, z, zs, 3)
+    await_bytes(z_in.at[0:7], z_sems.at[1, 0])
+    value = z_in[0].astype(F32)
+    for s in range(1, 8):
+        value = value + z_in[s].astype(F32)
+    z_done[z] = value.astype(BF16)
+    for s in range(1, 8):
+        send(z_done.at[z], z_done.at[z], z_sems.at[0, 1], z_sems.at[1, 1], zs[s][1], zs[s][0])
+    gain_total[...] = gain_done(9, 8, 3)
+    await_bytes(z_done.at[0:7], z_sems.at[1, 1])
+    bases = [core * half + axes[h][0] * large for h in (0, 1)]
+    for h in (0, 1):
+        at = bases[h] + swapped[h][0] * small
+        for j in (2 * h, 2 * h + 1):
+            both = jnp.concatenate([z_done[2 * j, 0:piece].astype(F32), z_done[2 * j + 1, 0:piece].astype(F32)], axis=0)
+            total[j, rows_at(at, small)] = both.astype(BF16)
+
+    def spread(base, size, pos, device, sems, h):
+        copies = {}
+        a, b = 2 * h, 2 * h + 1
+
+        def go(index, j, s, to):
+            part = total.at[j, rows_at(base + ring(pos, 4, s) * size, size)]
+            copies[index] = post(part, part, sems, (h, index), device[to])
+
+        go(0, a, 0, 1)
+        go(1, b, 0, 3)
+        go(2, b, 0, 1)
+        go(3, a, 0, 3)
+        return copies, go
+
+    def pass_on(state, h):
+        copies, go = state
+        copies[0].wait_recv()
+        go(4, 2 * h, 3, 1)
+        copies[1].wait_recv()
+        go(5, 2 * h + 1, 1, 3)
+
+    states = [spread(bases[h], small, swapped[h][0], swapped[h][1], gather2_sems, h) for h in (0, 1)]
+    for h in (0, 1):
+        pass_on(states[h], h)
+    for h in (0, 1):
+        for index in (2, 3, 4, 5):
+            states[h][0][index].wait_recv()
+
+    def to_sibling(k, h, s):
+        part = total.at[pair(h), rows_at(core * half + ring(axes[h][0], 4, s) * large, large)]
+        return post(part, part, last_sems, (h, k), (x, sibling))
+
+    states = [spread(core * half, large, axes[h][0], axes[h][1], gather1_sems, h) for h in (0, 1)]
+    last = [to_sibling(0, h, 0) for h in (0, 1)]
+    await_bytes(returned.at[0 : 16 * (patches - 1)], back_sems.at[1])
+    mine = rows_at(here * 16, 16)
+    returned[mine, :] = far_grad[mine, :]
+    for copy in rims:
+        copy.wait_recv()
+    width = node_partial.shape[1]
+    count = node_partial.shape[0]
+    back = jnp.concatenate(
+        [mm(gather_far(c, FAR * patches, False), returned[...]).astype(BF16) for c in range(width // 128)], axis=1
+    )
+    nodes = node_partial[...] + mm(send_one_hot(send_rows[...], count), back)
+    node_grad[0:RIM, :] = (nodes[0:RIM] + from_prev[...].astype(F32)).astype(BF16)
+    node_grad[RIM : count - RIM, :] = nodes[RIM : count - RIM].astype(BF16)
+    node_grad[count - RIM : count, :] = (nodes[count - RIM :] + from_next[...].astype(F32)).astype(BF16)
+    for h in (0, 1):
+        pass_on(states[h], h)
+    for h in (0, 1):
+        states[h][0][2].wait_recv()
+        last.append(to_sibling(1, h, 3))
+        states[h][0][3].wait_recv()
+        last.append(to_sibling(2, h, 1))
+    for h in (0, 1):
+        states[h][0][4].wait_recv()
+        states[h][0][5].wait_recv()
+        last.append(to_sibling(3, h, 2))
+    await_bytes(far_grad.at[0 : 16 * (patches - 1)], back_sems.at[0])
+    await_bytes(z_out.at[0:7], z_sems.at[0, 0])
+    await_bytes(z_done.at[0:7], z_sems.at[0, 1])
+    for copy in last:
+        copy.wait_recv()
+    for copy in pending:
+        copy.wait_send()
+
+
+def reduce_all(terms, gains, far_grad, low_grad, high_grad, node_partial, send_rows):
+    columns, rows, _ = terms.shape
+    count, width = node_partial.shape
+    patches = send_rows.shape[1]
+    half = rows // 2
+    large, small = half // 4, half // 16
+    whole = pl.BlockSpec(memory_space=VMEM)
+    dma = pltpu.SemaphoreType.DMA
+    return pl.pallas_call(
+        reduce_kernel,
+        out_shape=(
+            jax.ShapeDtypeStruct(terms.shape, BF16),
+            jax.ShapeDtypeStruct(gains.shape, F32),
+            jax.ShapeDtypeStruct((count, width), BF16),
+        ),
+        in_specs=[whole] * 7,
+        out_specs=(whole,) * 3,
+        scratch_shapes=[
+            VMEM((columns, half, 128), BF16),
+            VMEM((columns, half, 128), BF16),
+            VMEM((2, 6, large, 128), BF16),
+            VMEM((2, 6, small, 128), BF16),
+            VMEM((columns, large, 128), BF16),
+            VMEM((8, 64, 128), BF16),
+            VMEM((8, 64, 128), BF16),
+            VMEM((8, 64, 128), BF16),
+            VMEM((16 * patches, 128), BF16),
+            VMEM((RIM, width), BF16),
+            VMEM((RIM, width), BF16),
+            VMEM((17, 8, 128), F32),
+            dma((2, 2, 4)),
+            dma((2, 2, 6)),
+            dma((2, 2, 6)),
+            dma((2, 2)),
+            dma((2,)),
+            dma((2, 2)),
+            dma((2, 2, 6)),
+            dma((2, 2, 6)),
+            dma((2, 2, 4)),
+            dma((2, 4)),
+        ],
+        compiler_params=pltpu.CompilerParams(
+            collective_id=1, has_side_effects=True, vmem_limit_bytes=40 * 1024 * 1024
+        ),
+        name="reduce_all",
+    )(terms, gains, far_grad, low_grad, high_grad, node_partial, send_rows)
 
 
 def on_device(
     edge_latents, node_latents, edge_cotangent, node_cotangent, senders, receivers, send_rows,
     edge_first, edge_second, edge_gain, node_first, node_second, node_gain,
 ):
-    patches = lax.axis_size("patch")
     own = node_latents[0]
-    count, width = own.shape
-    outgoing = own[send_rows]
-    far = lax.all_to_all(outgoing, "patch", split_axis=0, concat_axis=0, tiled=True).reshape(patches * FAR, width)
-    low, high = with_halo_parts(own, "patch", RIM)
+    width = own.shape[1]
+    to_send = send_rows.T
+    low, high, far = exchange(own, to_send)
     edge_grad, node_partial, low_grad, high_grad, far_grad, terms, gains = local_layer(
         edge_latents[0], edge_cotangent[0], own, node_cotangent[0], low, high, far, senders, receivers,
         edge_first, edge_second, edge_gain, node_first, node_second, node_gain,
     )
-    from_next = from_behind(low_grad, "patch", -1).astype(F32)
-    from_prev = from_behind(high_grad, "patch", 1).astype(F32)
-    returned = lax.all_to_all(
-        far_grad.reshape(patches, FAR, width), "patch", split_axis=0, concat_axis=0, tiled=True
-    ).astype(F32)
-    node_total = node_partial + jnp.pad(from_prev, ((0, count - RIM), (0, 0)))
-    node_total = node_total + jnp.pad(from_next, ((count - RIM, 0), (0, 0)))
-    node_total = node_total + jax.ops.segment_sum(
-        returned.reshape(patches * FAR, width), send_rows.reshape(-1), num_segments=count
-    )
-    summed, gains = lax.psum((terms.astype(F32), gains), ("patch", "sample"))
-    summed = summed.astype(BF16)
-    flat = jnp.concatenate([summed[j] for j in range(4)], axis=1)
+    summed, gains, node_grad = reduce_all(terms, gains, far_grad, low_grad, high_grad, node_partial, to_send)
+    flat = jnp.concatenate([summed[j] for j in range(width // 128)], axis=1)
+    gains = gains.astype(BF16).reshape(2, width)
     return (
         edge_grad[None],
-        node_total.astype(BF16)[None],
+        node_grad[None],
         flat[: 3 * width],
         flat[3 * width : 4 * width],
         flat[4 * width : 6 * width],
         flat[6 * width :],
-        gains[0].astype(BF16),
-        gains[1].astype(BF16),
+        gains[0],
+        gains[1],
     )
 
 

time: 338 us -> 118 us (0.35)
  waiting for transfers between devices: 179 us -> 0 us
  blocking collectives: 81.8 us -> 0 us
  Pallas kernels: 15.9 us -> 97.2 us
  starting transfers between devices: 22.6 us -> 0 us
  between operations: 14.2 us -> 0.7 us
  other arithmetic: 6.55 us -> 2.62 us
    psum x1 -> x0, waiting for transfers between devices: 170 us -> none  [on_device(): summed, gains = lax.psum((terms.astype(F32), gains), ('patch', 'sample'))]
    psum x1 -> x0, blocking collectives: 81.8 us -> none  [on_device(): summed, gains = lax.psum((terms.astype(F32), gains), ('patch', 'sample'))]
    pallas_call x0 -> x2, Pallas kernels: none -> 80.6 us  [the longest x1 59.9 us: reduce_all(): pl.pallas_call(reduce_kernel, out_shape=(jax.ShapeDtypeStruct(terms.shape...]
    all_to_all x2 -> x0, starting transfers between devices: 18.9 us -> none  [the longest x1 13.2 us: on_device(): lax.all_to_all(outgoing, 'patch', split_axis=0, concat_axis=0, tiled=True)]
    all_to_all x2 -> x0, waiting for transfers between devices: 9.82 us -> none  [the longest x1 9.81 us: on_device(): lax.all_to_all(outgoing, 'patch', split_axis=0, concat_axis=0, tiled=True)]
    unnamed x25 -> x31, local copies, waits for them, and re-layouts: 7.1 us -> 14.8 us
    ppermute x4 -> x0, starting transfers between devices: 3.65 us -> none  [the longest x2 2.02 us: from_behind(): lax.ppermute(array, axis, [(i, (i + by) % size) for i in range(size)])]
  transfers between devices with their start and end apart: 7 -> 0, of which waited for: 2 -> 0; matrix products, arithmetic and copies ran while one was open for 2% -> 0% of each run, Pallas kernels for 0% -> 0%
where the time goes in v2:
time: 118 us; the launch traced here: 117 us
  Pallas kernels  97.2 us (82%)
  local copies, waits for them, and re-layouts  16.8 us (14%)
  other arithmetic  2.62 us (2%)
    pallas_call x1, Pallas kernels, reduce_all(): pl.pallas_call(reduce_kernel, out_shape=(jax.ShapeDtypeStruct(terms.shape...  59.9 us
    pallas_call x1, Pallas kernels, exchange(): pl.pallas_call(exchange_kernel, out_shape=(jax.ShapeDtypeStruct((RIM, wid...  20.8 us
    pallas_call x1, Pallas kernels, local_layer(): pl.pallas_call(layer_kernel, out_shape=shapes, in_specs=[whole] * 15, out...  16.6 us
    unnamed x31, local copies, waits for them, and re-layouts  14.8 us

profile of v2, /device:TPU:1, one launch (start us, length us, event | category | flops | bytes accessed | tf_op | source)
XLA Modules:
  0.0 117.4 jit_solution(1186899226036086724)
XLA Ops:
  0.6 0.0 copy-start.1
  0.6 0.9 copy-done.1
  1.6 0.0 copy-start.3
  1.6 0.7 copy-done.3
  2.3 20.8 %exchange.1 = (bf16[32,512]{1,0:T(8,128)(2,1)S(1)}, bf16[32,512]{1,0:T(8,128)(2,1)S(1)}, bf16[256,512]{1,0:T(8,128)(2,1)S(1)}) custom-call(bf16[256,512]{1,0:T(8,128)(2,1)S(1)} %bitcast.23, s32[4,64]{1,0:T(4,128)S(1)} %bitcast.26), custom_call_target="tpu_custom_call" | custom-call | tf_op jit(solution)/shard_map/exchange/pallas_call | solution.py:277
  23.1 0.0 copy-start.2
  23.1 0.9 copy-done.2
  24.0 0.0 copy-start.5
  24.0 1.2 %copy-done.5 = bf16[1,1024,512]{2,1,0:T(8,128)(2,1)S(1)} copy-done((bf16[1,1024,512]{2,1,0:T(8,128)(2,1)S(1)}, bf16[1,1024,512]{2,1,0:T(8,128)(2,1)}, u32[]{:S(2)}) %copy-start.5) | copy-done | bytes 1048600
  25.2 0.0 copy-start.6
  25.2 1.2 %copy-done.6 = bf16[1,1024,512]{2,1,0:T(8,128)(2,1)S(1)} copy-done((bf16[1,1024,512]{2,1,0:T(8,128)(2,1)S(1)}, bf16[1,1024,512]{2,1,0:T(8,128)(2,1)}, u32[]{:S(2)}) %copy-start.6) | copy-done | bytes 1048600
  26.5 0.0 copy-start.7
  26.5 1.2 %copy-done.7 = bf16[1024,512]{1,0:T(8,128)(2,1)S(1)} copy-done((bf16[1024,512]{1,0:T(8,128)(2,1)S(1)}, bf16[1024,512]{1,0:T(8,128)(2,1)}, u32[]{:S(2)}) %copy-start.7) | copy-done | bytes 1048600
  27.7 0.0 copy-start.8
  27.7 1.0 copy-done.8
  28.7 0.0 copy-start.9
  28.7 1.0 copy-done.9
  29.8 0.0 copy-start.10
  29.8 0.9 copy-done.10
  30.7 0.0 copy-start.11
  30.7 0.7 copy-done.11
  31.4 0.0 copy-start.12
  31.4 0.7 copy-done.12
  32.1 0.0 copy-start.13
  32.1 0.7 copy-done.13
  32.8 0.0 copy-start.14
  32.8 0.7 copy-done.14
  33.5 0.0 copy-start.4
  33.5 16.6 %local_layer.1 = (bf16[1024,512]{1,0:T(8,128)(2,1)}, f32[256,512]{1,0:T(8,128)S(1)}, bf16[32,512]{1,0:T(8,128)(2,1)S(1)}, bf16[32,512]{1,0:T(8,128)(2,1)S(1)}, b...) custom-call(bf16[1024,512]{1,0:T(8,128)(2,1)S(1)} %bitcast.28, ...), custom_call_target="tpu_custom_call" | custom-call | flops 8000000000 | bytes 20000000 | tf_op jit(solution)/shard_map/local_layer/pallas_call | solution.py:179
  50.0 0.0 copy-done.4
  50.0 0.0 copy-start
  50.0 2.0 %copy-done = bf16[4,3584,128]{2,1,0:T(8,128)(2,1)S(1)} copy-done((bf16[4,3584,128]{2,1,0:T(8,128)(2,1)S(1)}, bf16[4,3584,128]{2,1,0:T(8,128)(2,1)}, u32[]{:S(2)}) %copy-start) | copy-done | bytes 3670040
  52.1 59.9 %reduce_all.1 = (bf16[4,3584,128]{2,1,0:T(8,128)(2,1)S(1)}, f32[8,128]{1,0:T(8,128)S(1)}, bf16[256,512]{1,0:T(8,128)(2,1)S(1)}) custom-call(bf16[4,3584,128]{2,1,0:T(8,128)(2,1)S(1)} %copy-done, f32[8,128]{1,0:T(8,128)S(1)} %get-tuple-element.26.gains, bf16[1024,128]{1,0:T(8,128)(2,1)S(1)} %get-tuple-element.27.far_grad, ...), custom_call_target="tpu_custom_call" | custom-call | tf_op jit(solution)/shard_map/reduce_all/pallas_call | solution.py:553
  112.0 0.2 slice_bitcast_fusion.3
  112.2 0.4 pad_maximum_fusion
  112.7 1.2 %slice.42 = bf16[1536,512]{1,0:T(8,128)(2,1)} slice(bf16[3584,512]{1,0:T(8,128)(2,1)S(1)} %pad_maximum_fusion), slice={[0:1536], [0:512]} | slice | bytes 3145728 | tf_op jit(solution)/shard_map/slice | solution.py:611
  113.9 1.1 pad_maximum_fusion.2
  115.0 1.1 pad_maximum_fusion.1
  116.1 0.6 slice_bitcast_fusion.4
  116.7 0.7 copy.22
  (1 shorter events, 0.0 us)
Async XLA Ops:
  0.6 1.0 copy-start.1
  1.6 0.7 copy-start.3
  23.1 1.0 copy-start.2
  24.0 1.2 %copy-start.5 = (bf16[1,1024,512]{2,1,0:T(8,128)(2,1)S(1)}, bf16[1,1024,512]{2,1,0:T(8,128)(2,1)}, u32[]{:S(2)}) copy-start(bf16[1,1024,512]{2,1,0:T(8,128)(2,1)} %param.13) | copy-start | bytes 3145732
  25.2 1.2 %copy-start.6 = (bf16[1,1024,512]{2,1,0:T(8,128)(2,1)S(1)}, bf16[1,1024,512]{2,1,0:T(8,128)(2,1)}, u32[]{:S(2)}) copy-start(bf16[1,1024,512]{2,1,0:T(8,128)(2,1)} %param.15) | copy-start | bytes 3145732
  26.5 1.2 %copy-start.7 = (bf16[1024,512]{1,0:T(8,128)(2,1)S(1)}, bf16[1024,512]{1,0:T(8,128)(2,1)}, u32[]{:S(2)}) copy-start(bf16[1024,512]{1,0:T(8,128)(2,1)} %nw1.1) | copy-start | bytes 3145732
  27.7 1.0 copy-start.8
  28.7 1.0 copy-start.9
  29.8 0.9 copy-start.10
  30.7 0.7 copy-start.11
  31.4 0.7 copy-start.12
  32.1 0.7 copy-start.13
  32.8 0.7 copy-start.14
  33.5 16.6 %copy-start.4 = (s32[64,4]{0,1:T(4,128)S(1)}, s32[64,4]{0,1:T(4,128)}, u32[]{:S(2)}) copy-start(s32[64,4]{0,1:T(4,128)} %param.19) | copy-start | bytes 3076
  50.0 2.0 %copy-start = (bf16[4,3584,128]{2,1,0:T(8,128)(2,1)S(1)}, bf16[4,3584,128]{2,1,0:T(8,128)(2,1)}, u32[]{:S(2)}) copy-start(bf16[4,3584,128]{2,1,0:T(8,128)(2,1)} %get-tuple-element.25.terms) | copy-start | bytes 11010052

commit v3 on v1

v3 whole, which is shorter than its diff:
```python
import functools

import jax
import jax.numpy as jnp
from jax import lax
from jax.experimental import pallas as pl
from jax.experimental.pallas import tpu as pltpu
from jax.sharding import PartitionSpec as P

RIM = 32
FAR = 4
MESH = pl.DeviceIdType.MESH
F32 = jnp.float32
BF16 = jnp.bfloat16
VMEM = pltpu.VMEM


def mm(a, b):
    return lax.dot_general(a, b, (((1,), (0,)), ((), ())), preferred_element_type=F32)


def mm_nt(a, b):
    return lax.dot_general(a, b, (((1,), (1,)), ((), ())), preferred_element_type=F32)


def mm_tn(a, b):
    return lax.dot_general(a, b, (((0,), (0,)), ((), ())), preferred_element_type=F32)


def one_hot_cols(col, width, first=0):
    parts = []
    lanes = lax.broadcasted_iota(jnp.int32, col.shape, 1) + first
    for start in range(0, width, 128):
        size = min(128, width - start)
        hit = (col == lanes + start).astype(F32).astype(BF16)
        parts.append(hit if size == 128 else hit[:, :size])
    return jnp.concatenate(parts, axis=1) if len(parts) > 1 else parts[0]


def one_hot_rows(row, height):
    ids = lax.broadcasted_iota(jnp.int32, (height, row.shape[1]), 0)
    return (ids == row).astype(F32).astype(BF16)


def lane_block(packed, c):
    return (lax.broadcasted_iota(jnp.int32, packed.shape, 0) // FAR) % 4 == c


def spread(rows, by_patch):
    at = lax.broadcasted_iota(jnp.int32, (4 * rows, rows), 0)
    col = lax.broadcasted_iota(jnp.int32, (4 * rows, rows), 1)
    patch, r = at // 16, at % 4
    return (col == (patch * FAR + r if by_patch else r * (rows // FAR) + patch)).astype(F32).astype(BF16)


def unspread(rows, by_patch):
    at = lax.broadcasted_iota(jnp.int32, (rows, 4 * rows), 1)
    row = lax.broadcasted_iota(jnp.int32, (rows, 4 * rows), 0)
    patch, r = at // 16, at % 4
    return (row == (patch * FAR + r if by_patch else r * (rows // FAR) + patch)).astype(F32).astype(BF16)


def pack(values, by_patch):
    wide = mm(spread(values.shape[0], by_patch), values)
    packed = wide[:, 0:128]
    for c in (1, 2, 3):
        packed = jnp.where(lane_block(packed, c), wide[:, 128 * c : 128 * c + 128], packed)
    return packed.astype(BF16)


def unpack(packed, by_patch):
    values = packed.astype(F32)
    wide = jnp.concatenate([jnp.where(lane_block(values, c), values, 0.0).astype(BF16) for c in range(4)], axis=1)
    return mm(unspread(packed.shape[0] // 4, by_patch), wide).astype(BF16)


def send_one_hot(send_rows, count):
    return jnp.concatenate([one_hot_rows(send_rows[r : r + 1, :], count) for r in range(FAR)], axis=1)


def normalize(values):
    center = values - jnp.mean(values, axis=1, keepdims=True)
    spread = jnp.mean(center * center, axis=1, keepdims=True)
    scale = lax.rsqrt(spread + 1e-05)
    return (center * scale, scale)


def normalize_back(grads, normed, scale):
    first = jnp.mean(grads, axis=1, keepdims=True)
    second = jnp.mean(grads * normed, axis=1, keepdims=True)
    return (grads - first - normed * second) * scale


def place():
    here = lax.axis_index("patch")
    return here, lax.axis_index("sample"), lax.div(here, 16), lax.rem(lax.div(here, 2), 8), lax.rem(here, 2)


def ring(here, count, step):
    return lax.rem(here + (step + count) % count, count)


def signal(patch, sample):
    pl.semaphore_signal(
        pltpu.get_barrier_semaphore(), inc=1, device_id={"patch": patch, "sample": sample}, device_id_type=MESH
    )


def send(src, dst, send_sem, recv_sem, patch, sample):
    copy = pltpu.make_async_remote_copy(
        src_ref=src, dst_ref=dst, send_sem=send_sem, recv_sem=recv_sem,
        device_id={"patch": patch, "sample": sample}, device_id_type=MESH,
    )
    copy.start()
    return copy


def await_bytes(ref, sem):
    pltpu.make_async_copy(ref, ref, sem).wait()


def rows_at(start, size, align=16):
    return pl.ds(pl.multiple_of(start, align), size)


def reduction(terms, total, where, scratch, pending):
    x, y, z, core, here, xs, ys, zs = where
    core_in, summed, first_in, second, second_in, z_out, z_in, z_done, sems, z_sems = scratch
    half = terms.shape[1] // 2
    large, small = half // 4, half // 16
    piece = small // 2
    sibling = here + 1 - 2 * core
    outer = ((x, xs), (y, ys))
    inner = ((y, ys), (x, xs))
    both = (0, 1)

    def post(src, dst, index, device):
        copy = send(src, dst, sems.at[(0,) + index], sems.at[(1,) + index], device[1], device[0])
        pending.append(copy)
        return copy

    def pair(h):
        return slice(2 * h, 2 * h + 2)

    def chunk(axis, s, size):
        return ring(axis[0], 4, s) * size

    copies = {}
    for k, s in enumerate((2, 1, 3, 0)):
        for h in both:
            at = chunk(outer[h], s, large)
            copies[h, s] = post(
                terms.at[pair(h), rows_at((1 - core) * half + at, large)],
                core_in.at[pair(h), rows_at(at, large)], (0, h, s), (x, sibling),
            )
    yield

    def core_ready(h, s):
        copies[h, s].wait_recv()
        at = chunk(outer[h], s, large)
        for j in (2 * h, 2 * h + 1):
            mine = terms[j, rows_at(core * half + at, large)].astype(F32)
            summed[j, rows_at(at, large)] = (mine + core_in[j, rows_at(at, large)].astype(F32)).astype(BF16)

    first = {}
    for s in (2, 1, 3):
        for h in both:
            core_ready(h, s)
            first[h, s] = post(
                summed.at[pair(h), rows_at(chunk(outer[h], s, large), large)], first_in.at[h, s - 1],
                (1, h, s), outer[h][1][s],
            )
    for h in both:
        core_ready(h, 0)
    yield

    def collect(h, j, source, at, size, landing):
        value = source[2 * h + j, rows_at(at, size)].astype(F32)
        for s in (1, 2, 3):
            value = value + landing[h, s - 1, j].astype(F32)
        return value

    then = {}
    for h in both:
        for s in (1, 2, 3):
            first[h, s].wait_recv()
        for j in both:
            second[2 * h + j] = collect(h, j, summed, chunk(outer[h], 0, large), large, first_in).astype(BF16)
        for s in (2, 1, 3):
            then[h, s] = post(
                second.at[pair(h), rows_at(chunk(inner[h], s, small), small)], second_in.at[h, s - 1],
                (2, h, s), inner[h][1][s],
            )
    yield
    if z_out.shape[1] > piece:
        z_out[...] = jnp.zeros(z_out.shape, BF16)
    for h in both:
        for s in (1, 2, 3):
            then[h, s].wait_recv()
        for j in both:
            value = collect(h, j, second, chunk(inner[h], 0, small), small, second_in).astype(BF16)
            for k in both:
                z_out[(2 * h + j) * 2 + k, 0:piece, :] = value[piece * k : piece * (k + 1), :]
    for s in (4, 3, 5, 2, 6, 1, 7):
        send(z_out.at[ring(z, 8, s)], z_in.at[z], z_sems.at[0, 0], z_sems.at[1, 0], zs[s][1], zs[s][0])
    z_in[z] = z_out[z]
    yield
    await_bytes(z_in.at[0:7], z_sems.at[1, 0])
    value = z_in[0].astype(F32)
    for s in range(1, 8):
        value = value + z_in[s].astype(F32)
    z_done[z] = value.astype(BF16)
    for s in (4, 3, 5, 2, 6, 1, 7):
        send(z_done.at[z], z_done.at[z], z_sems.at[0, 1], z_sems.at[1, 1], zs[s][1], zs[s][0])
    yield
    await_bytes(z_done.at[0:7], z_sems.at[1, 1])
    back = {}

    def share(h, base, axis, size, stage):
        part = total.at[pair(h), rows_at(base + axis[0] * size, size)]
        for s in (2, 1, 3):
            back[stage, h, s] = post(part, part, (stage, h, s), axis[1][s])

    bases = [core * half + chunk(outer[h], 0, large) for h in both]
    for h in both:
        at = bases[h] + chunk(inner[h], 0, small)
        for j in (2 * h, 2 * h + 1):
            joined = jnp.concatenate([z_done[2 * j + k, 0:piece].astype(F32) for k in both], axis=0)
            total[j, rows_at(at, small)] = joined.astype(BF16)
        share(h, bases[h], inner[h], small, 3)
    yield
    for h in both:
        for s in (1, 2, 3):
            back[3, h, s].wait_recv()
        share(h, core * half, outer[h], large, 4)
    last = []

    def to_sibling(h, s):
        part = total.at[pair(h), rows_at(core * half + chunk(outer[h], -s, large), large)]
        last.append(post(part, part, (5, h, s), (x, sibling)))

    for h in both:
        to_sibling(h, 0)
    yield
    for s in (1, 3, 2):
        for h in both:
            back[4, h, s].wait_recv()
            to_sibling(h, s)
    yield
    for copy in last:
        copy.wait_recv()
    await_bytes(z_out.at[0:7], z_sems.at[0, 0])
    await_bytes(z_done.at[0:7], z_sems.at[0, 1])


def gain_reduction(value, result, where, slots, sems):
    x, y, z, core, here, xs, ys, zs = where
    cores = [(x, here), (x, here + 1 - 2 * core)]
    base = 0
    for index, (count, pos, devices) in enumerate(((2, core, cores), (4, x, xs), (4, y, ys), (8, z, zs))):
        slots[base + pos] = value
        for s in range(1, count):
            mine = slots.at[base + pos]
            send(mine, mine, sems.at[0, index], sems.at[1, index], devices[s][1], devices[s][0])
        yield
        await_bytes(slots.at[base : base + count - 1], sems.at[1, index])
        await_bytes(slots.at[base : base + count - 1], sems.at[0, index])
        value = slots[base]
        for s in range(1, count):
            value = value + slots[base + s]
        base += count
    result[...] = value


def advance(step):
    next(step, None)


def layer_kernel(
    nodes, send_rows, senders, receivers, gain, ngain, lat_in, cot_in, ncot_in, w1_in, w2_in, nw1_in, nw2_in,
    edge_grad, node_grad, edge_total, node_total, gain_total,
    lat, cot, ncot, w1, w2, nw1, nw2, others, packed, incoming, far_grad, returned, rim_grad, from_rims,
    onehot, projected, act, slope, hat, scale, raw_grad, pre_grad, node_partial, edge_terms, node_terms, slots, *rest,
):
    edge_scratch, node_scratch = rest[0:10], rest[10:20]
    load_sems, far_sems, rim_sems, back_sems, back_rim_sems, gain_sems = rest[20:]
    here, x, y, z, core = place()
    edges, width = lat.shape
    count = nodes.shape[0]
    patches = send_rows.shape[1]
    outside = others.shape[0]
    rows = count + outside
    block = 256
    xs = [(x, here)] + [(ring(x, 4, s), here) for s in (1, 2, 3)]
    ys = [(x, here)] + [(x, ring(y, 4, s) * 16 + z * 2 + core) for s in (1, 2, 3)]
    zs = [(x, here)] + [(x, y * 16 + ring(z, 8, s) * 2 + core) for s in range(1, 8)]
    where = (x, y, z, core, here, xs, ys, zs)
    behind, ahead = ring(here, patches, -1), ring(here, patches, 1)

    loads = [
        pltpu.make_async_copy(src, dst, load_sems.at[k])
        for k, (src, dst) in enumerate(
            ((w1_in, w1), (lat_in, lat), (w2_in, w2), (nw1_in, nw1), (nw2_in, nw2), (ncot_in, ncot), (cot_in, cot))
        )
    ]
    for copy in loads:
        copy.start()

    def greet(k, carry):
        signal(lax.rem(here + k, patches), x)
        return carry

    lax.fori_loop(1, patches, greet, 0)
    for s in (1, 2, 3):
        signal(here, ring(x, 4, s))
    spread_nodes = send_one_hot(send_rows[...], count)
    packed[...] = pack(mm_tn(spread_nodes, nodes[...]).astype(BF16), False)
    pl.semaphore_wait(pltpu.get_barrier_semaphore(), patches + 2)
    rims = (
        send(nodes.at[count - RIM : count], others.at[0:RIM], rim_sems.at[0, 0], rim_sems.at[1, 0], ahead, x),
        send(nodes.at[0:RIM], others.at[RIM : 2 * RIM], rim_sems.at[0, 1], rim_sems.at[1, 1], behind, x),
    )

    def push(src, dst, sems):
        def one(k, carry):
            to = lax.rem(here + k, patches)
            send(src.at[rows_at(to * 16, 16)], dst.at[rows_at(here * 16, 16)], sems.at[0], sems.at[1], to, x)
            return carry

        lax.fori_loop(1, patches, one, 0)

    mine = rows_at(here * 16, 16)
    all_but_mine = slice(0, 16 * (patches - 1))
    push(packed, incoming, far_sems)

    send_row, recv_row = senders[...], receivers[...]
    table_row = jnp.where(send_row < RIM, send_row + count, jnp.where(send_row < RIM + count, send_row - RIM, send_row))
    send_col = jnp.transpose(jnp.broadcast_to(table_row, (128, edges)))
    recv_col = jnp.transpose(jnp.broadcast_to(recv_row, (128, edges)))
    onehot[:, 0:count] = one_hot_cols(send_col, count)
    onehot[:, count : 2 * count] = one_hot_cols(recv_col, count)
    onehot[:, 2 * count : 2 * count + outside] = one_hot_cols(send_col, outside, count)
    recv_rows = one_hot_rows(recv_row, count)
    loads[0].wait()
    projected[0:count, :] = mm(nodes[...], w1[width : 2 * width, :]).astype(BF16)
    projected[count : 2 * count, :] = mm(nodes[...], w1[2 * width :, :]).astype(BF16)
    loads[1].wait()
    for start in range(0, edges, block):
        part = slice(start, start + block)
        slope[part, :] = mm(lat[part, :], w1[0:width, :]) + mm(onehot[part, 0 : 2 * count], projected[0 : 2 * count, :])

    for copy in rims:
        copy.wait_recv()
    incoming[mine, :] = packed[mine, :]
    await_bytes(incoming.at[all_but_mine], far_sems.at[1])
    others[2 * RIM :, :] = unpack(incoming[...], True)
    projected[2 * count : 2 * count + outside, :] = mm(others[...], w1[width : 2 * width, :]).astype(BF16)
    loads[2].wait()
    edge_gain = gain[...]
    inflow = jnp.zeros((count, width), F32)
    for start in range(0, edges, block):
        part = slice(start, start + block)
        pre = slope[part, :] + mm(onehot[part, 2 * count :], projected[2 * count :, :])
        sig = jax.nn.sigmoid(pre)
        acted = (pre * sig).astype(BF16)
        act[part, :] = acted
        slope[part, :] = sig * (1.0 + pre * (1.0 - sig))
        normed, inv = normalize(mm(acted, w2[...]))
        hat[part, :] = normed
        scale[part, :] = inv
        inflow = inflow + mm(recv_rows[:, part], (normed * edge_gain).astype(BF16))
    inflow = inflow.astype(BF16)
    for copy in loads[3:]:
        copy.wait()
    node_pre = mm(nodes[...], nw1[0:width, :]) + mm(inflow, nw1[width:, :])
    node_sig = jax.nn.sigmoid(node_pre)
    node_act = (node_pre * node_sig).astype(BF16)
    node_hat, node_scale = normalize(mm(node_act, nw2[...]))
    upstream = ncot[...].astype(F32)
    node_gain_grad = jnp.sum(upstream * node_hat, axis=0, keepdims=True)
    node_raw_grad = normalize_back(upstream * ngain[...], node_hat, node_scale).astype(BF16)
    node_act_grad = mm_nt(node_raw_grad, nw2[...])
    node_pre_grad = (node_act_grad * node_sig * (1.0 + node_pre * (1.0 - node_sig))).astype(BF16)

    def put(terms, row, value):
        for j in range(width // 128):
            terms[j, row : row + value.shape[0], :] = value[:, 128 * j : 128 * j + 128].astype(BF16)

    put(node_terms, 0, mm_tn(nodes[...], node_pre_grad))
    put(node_terms, width, mm_tn(inflow, node_pre_grad))
    put(node_terms, 2 * width, mm_tn(node_act, node_raw_grad))
    pending = []
    node_sum = reduction(node_terms, node_total, where, node_scratch, pending)
    advance(node_sum)
    node_partial[...] = upstream + mm_nt(node_pre_grad, nw1[0:width, :])
    inflow_grad = mm_nt(node_pre_grad, nw1[width:, :]).astype(BF16)
    gain_grad = jnp.zeros((1, width), F32)
    for start in range(0, edges, block):
        part = slice(start, start + block)
        edge_cot = cot[part, :].astype(F32)
        normed = hat[part, :]
        update_grad = edge_cot + mm(onehot[part, count : 2 * count], inflow_grad)
        gain_grad = gain_grad + jnp.sum(update_grad * normed, axis=0, keepdims=True)
        back = normalize_back(update_grad * edge_gain, normed, scale[part, :]).astype(BF16)
        raw_grad[part, :] = back
        pre_back = (mm_nt(back, w2[...]) * slope[part, :]).astype(BF16)
        pre_grad[part, :] = pre_back
        edge_grad[part, :] = (edge_cot + mm_nt(pre_back, w1[0:width, :])).astype(BF16)
        if start == 0:
            advance(node_sum)
    all_pre = pre_grad[...]
    put(edge_terms, 3 * width, mm_tn(act[...], raw_grad[...]))
    put(edge_terms, 0, mm_tn(lat[...], all_pre))
    send_sum = mm(one_hot_rows(table_row, rows), all_pre).astype(BF16)
    recv_sum = mm(recv_rows, all_pre).astype(BF16)
    put(edge_terms, width, mm_tn(nodes[...], send_sum[0:count]) + mm_tn(others[...], send_sum[count:]))
    put(edge_terms, 2 * width, mm_tn(nodes[...], recv_sum))
    edge_sum = reduction(edge_terms, edge_total, where, edge_scratch, pending)
    advance(edge_sum)
    advance(node_sum)
    gain_rows = [gain_grad[:, 128 * j : 128 * j + 128] for j in range(width // 128)]
    gain_rows += [node_gain_grad[:, 128 * j : 128 * j + 128] for j in range(width // 128)]
    gain_sum = gain_reduction(jnp.concatenate(gain_rows, axis=0), gain_total, where, slots, gain_sems)
    advance(gain_sum)
    other_grad = mm_nt(send_sum[count:], w1[width : 2 * width, :]).astype(BF16)
    rim_grad[...] = other_grad[0 : 2 * RIM]
    back_rims = (
        send(rim_grad.at[RIM : 2 * RIM], from_rims.at[0:RIM], back_rim_sems.at[0, 0], back_rim_sems.at[1, 0], ahead, x),
        send(rim_grad.at[0:RIM], from_rims.at[RIM : 2 * RIM], back_rim_sems.at[0, 1], back_rim_sems.at[1, 1], behind, x),
    )
    advance(edge_sum)
    far_grad[...] = pack(other_grad[2 * RIM :], True)
    push(far_grad, returned, back_sems)
    node_partial[...] += mm_nt(send_sum[0:count], w1[width : 2 * width, :]) + mm_nt(recv_sum, w1[2 * width :, :])
    advance(node_sum)
    advance(gain_sum)
    returned[mine, :] = far_grad[mine, :]
    advance(edge_sum)
    advance(node_sum)
    advance(gain_sum)
    for copy in back_rims:
        copy.wait_recv()
    await_bytes(returned.at[all_but_mine], back_sems.at[1])
    nodes_done = node_partial[...] + mm(spread_nodes, unpack(returned[...], False))
    node_grad[0:RIM, :] = (nodes_done[0:RIM] + from_rims[0:RIM].astype(F32)).astype(BF16)
    node_grad[RIM : count - RIM, :] = nodes_done[RIM : count - RIM].astype(BF16)
    node_grad[count - RIM : count, :] = (nodes_done[count - RIM :] + from_rims[RIM : 2 * RIM].astype(F32)).astype(BF16)
    advance(edge_sum)
    advance(node_sum)
    advance(gain_sum)
    for _ in range(8):
        advance(edge_sum)
        advance(node_sum)
    advance(gain_sum)
    for copy in rims + back_rims:
        copy.wait_send()
    await_bytes(packed.at[all_but_mine], far_sems.at[0])
    await_bytes(far_grad.at[all_but_mine], back_sems.at[0])
    for copy in pending:
        copy.wait_send()


def place_kernel(
    edge_total, node_total, edge_in, node_in, gains, first, second, nfirst, nsecond, edge_out, node_out, gain_out, ngain_out,
    edge_in_v, node_in_v, edge_v, rows_v, nfirst_v, nsecond_v, first_v, second_v, in_sems, out_sems,
):
    width = first.shape[1]
    starts = []
    for k, (src, dst) in enumerate(
        ((edge_total, edge_in_v), (node_total, node_in_v), (edge_in, edge_v), (node_in, rows_v))
    ):
        starts.append(pltpu.make_async_copy(src, dst, in_sems.at[k]))
        starts[-1].start()
    ends = []

    def out(src, dst):
        ends.append(pltpu.make_async_copy(src, dst, out_sems.at[len(ends)]))
        ends[-1].start()

    def relay(source, first, dst):
        rows = dst.shape[0]
        for j in range(width // 128):
            dst[:, 128 * j : 128 * j + 128] = source[j, first : first + rows, :]

    for j in range(width // 128):
        cols = slice(128 * j, 128 * j + 128)
        gain_out[cols] = gains[j, :].astype(BF16)
        ngain_out[cols] = gains[4 + j, :].astype(BF16)
    starts[0].wait()
    relay(edge_in_v, 0, first_v)
    out(first_v, first)
    relay(edge_in_v, 3 * width, second_v)
    out(second_v, second)
    starts[1].wait()
    relay(node_in_v, 0, nfirst_v)
    out(nfirst_v, nfirst)
    relay(node_in_v, 2 * width, nsecond_v)
    out(nsecond_v, nsecond)
    starts[2].wait()
    out(edge_v, edge_out)
    starts[3].wait()
    out(rows_v, node_out)
    for copy in ends:
        copy.wait()


def place_results(edge_total, node_total, edge_grad, node_grad, gains):
    width = edge_grad.shape[1]
    anywhere, whole = pl.BlockSpec(memory_space=pl.ANY), pl.BlockSpec(memory_space=VMEM)
    return pl.pallas_call(
        place_kernel,
        out_shape=tuple(
            jax.ShapeDtypeStruct(shape, BF16)
            for shape in (
                (3 * width, width), (width, width), (2 * width, width), (width, width),
                edge_grad.shape, node_grad.shape, (width,), (width,),
            )
        ),
        in_specs=[anywhere] * 4 + [whole],
        out_specs=(anywhere,) * 6 + (whole,) * 2,
        scratch_shapes=[
            VMEM(edge_total.shape, BF16),
            VMEM(node_total.shape, BF16),
            VMEM(edge_grad.shape, BF16),
            VMEM(node_grad.shape, BF16),
            VMEM((2 * width, width), BF16),
            VMEM((width, width), BF16),
            VMEM((3 * width, width), BF16),
            VMEM((width, width), BF16),
            pltpu.SemaphoreType.DMA((4,)),
            pltpu.SemaphoreType.DMA((6,)),
        ],
        compiler_params=pltpu.CompilerParams(vmem_limit_bytes=56 * 1024 * 1024),
        name="place_results",
    )(edge_total, node_total, edge_grad, node_grad, gains)


def reduction_scratch(total):
    half = total // 2
    large, small = half // 4, half // 16
    padded = -(-(small // 2) // 16) * 16
    dma = pltpu.SemaphoreType.DMA
    return [
        VMEM((4, half, 128), BF16),
        VMEM((4, half, 128), BF16),
        VMEM((2, 3, 2, large, 128), BF16),
        VMEM((4, large, 128), BF16),
        VMEM((2, 3, 2, small, 128), BF16),
        VMEM((8, padded, 128), BF16),
        VMEM((8, padded, 128), BF16),
        VMEM((8, padded, 128), BF16),
        dma((2, 6, 2, 4)),
        dma((2, 2)),
    ]


def layer(lat, cot, nodes, ncot, senders, receivers, send_rows, w1, w2, gain, nw1, nw2, ngain):
    edges, width = lat.shape
    count = nodes.shape[0]
    patches = send_rows.shape[1]
    outside = 2 * RIM + FAR * patches
    anywhere, whole = pl.BlockSpec(memory_space=pl.ANY), pl.BlockSpec(memory_space=VMEM)
    dma = pltpu.SemaphoreType.DMA
    packed = VMEM((16 * patches, 128), BF16)
    return pl.pallas_call(
        layer_kernel,
        out_shape=(
            jax.ShapeDtypeStruct((edges, width), BF16),
            jax.ShapeDtypeStruct((count, width), BF16),
            jax.ShapeDtypeStruct((4, 4 * width, 128), BF16),
            jax.ShapeDtypeStruct((4, 3 * width, 128), BF16),
            jax.ShapeDtypeStruct((8, 128), F32),
        ),
        in_specs=[whole] * 6 + [anywhere] * 7,
        out_specs=(whole,) * 5,
        scratch_shapes=[
            VMEM(lat.shape, BF16),
            VMEM(cot.shape, BF16),
            VMEM(ncot.shape, BF16),
            VMEM(w1.shape, BF16),
            VMEM(w2.shape, BF16),
            VMEM(nw1.shape, BF16),
            VMEM(nw2.shape, BF16),
            VMEM((outside, width), BF16),
            packed,
            packed,
            packed,
            packed,
            VMEM((2 * RIM, width), BF16),
            VMEM((2 * RIM, width), BF16),
            VMEM((edges, 2 * count + outside), BF16),
            VMEM((2 * count + outside, width), BF16),
            VMEM((edges, width), BF16),
            VMEM((edges, width), F32),
            VMEM((edges, width), F32),
            VMEM((edges, 1), F32),
            VMEM((edges, width), BF16),
            VMEM((edges, width), BF16),
            VMEM((count, width), F32),
            VMEM((4, 4 * width, 128), BF16),
            VMEM((4, 3 * width, 128), BF16),
            VMEM((18, 8, 128), F32),
        ]
        + reduction_scratch(4 * width)
        + reduction_scratch(3 * width)
        + [dma((7,)), dma((2,)), dma((2, 2)), dma((2,)), dma((2, 2)), dma((2, 4))],
        compiler_params=pltpu.CompilerParams(
            collective_id=0, has_side_effects=True, vmem_limit_bytes=56 * 1024 * 1024
        ),
        name="layer",
    )(
        nodes, send_rows, senders.reshape(1, edges), receivers.reshape(1, edges),
        gain.reshape(1, width), ngain.reshape(1, width), lat, cot, ncot, w1, w2, nw1, nw2,
    )


def on_device(
    edge_latents, node_latents, edge_cotangent, node_cotangent, senders, receivers, send_rows,
    edge_first, edge_second, edge_gain, node_first, node_second, node_gain,
):
    width = edge_first.shape[1]
    edge_grad, node_grad, edge_total, node_total, gains = layer(
        edge_latents[0], edge_cotangent[0], node_latents[0], node_cotangent[0], senders, receivers, send_rows.T,
        edge_first, edge_second, edge_gain, node_first, node_second, node_gain,
    )
    first, second, nfirst, nsecond, edge_grad, node_grad, gain_grad, ngain_grad = place_results(
        edge_total, node_total, edge_grad, node_grad, gains
    )
    return (
        edge_grad[None], node_grad[None], first, second, nfirst, nsecond,
        gain_grad, ngain_grad,
    )


def solution(mesh):
    return jax.shard_map(
        on_device,
        mesh=mesh,
        in_specs=(
            P("sample", "patch", None), P("sample", "patch", None), P("sample", "patch", None),
            P("sample", "patch", None), P("patch"), P("patch"), P("patch", None),
            P(), P(), P(), P(), P(), P(),
        ),
        out_specs=(P("sample", "patch", None), P("sample", "patch", None), P(), P(), P(), P(), P(), P()),
        check_vma=False,
    )
```

time: 338 us -> 85 us (0.25)
  waiting for transfers between devices: 179 us -> 0 us
  blocking collectives: 81.8 us -> 0 us
  Pallas kernels: 15.9 us -> 84 us
  starting transfers between devices: 22.6 us -> 0 us
  local copies, waits for them, and re-layouts: 16.1 us -> 0 us
  between operations: 14.2 us -> 0.81 us
  other arithmetic: 6.55 us -> 0 us
    psum x1 -> x0, waiting for transfers between devices: 170 us -> none  [on_device(): summed, gains = lax.psum((terms.astype(F32), gains), ('patch', 'sample'))]
    psum x1 -> x0, blocking collectives: 81.8 us -> none  [on_device(): summed, gains = lax.psum((terms.astype(F32), gains), ('patch', 'sample'))]
    pallas_call x1 -> x2, Pallas kernels: 15.9 us -> 84 us  [the longest x1 78.6 us: layer(): pl.pallas_call(layer_kernel, out_shape=(jax.ShapeDtypeStruct((edges, widt...]
    all_to_all x2 -> x0, starting transfers between devices: 18.9 us -> none  [the longest x1 13.2 us: on_device(): lax.all_to_all(outgoing, 'patch', split_axis=0, concat_axis=0, tiled=True)]
    all_to_all x2 -> x0, waiting for transfers between devices: 9.82 us -> none  [the longest x1 9.81 us: on_device(): lax.all_to_all(outgoing, 'patch', split_axis=0, concat_axis=0, tiled=True)]
    unnamed x25 -> x0, local copies, waits for them, and re-layouts: 7.1 us -> none
    ppermute x4 -> x0, starting transfers between devices: 3.65 us -> none  [the longest x2 2.02 us: from_behind(): lax.ppermute(array, axis, [(i, (i + by) % size) for i in range(size)])]
  transfers between devices with their start and end apart: 7 -> 0, of which waited for: 2 -> 0; matrix products, arithmetic and copies ran while one was open for 2% -> 0% of each run, Pallas kernels for 0% -> 0%
where the time goes in v3:
time: 85 us; the launch traced here: 84.8 us
  Pallas kernels  84 us (99%)
    pallas_call x1, Pallas kernels, layer(): pl.pallas_call(layer_kernel, out_shape=(jax.ShapeDtypeStruct((edges, widt...  78.6 us
    pallas_call x1, Pallas kernels, place_results(): pl.pallas_call(place_kernel, out_shape=tuple((jax.ShapeDtypeStruct(shape,...  5.46 us

profile of v3, /device:TPU:1, one launch (start us, length us, event | category | flops | bytes accessed | tf_op | source)
XLA Modules:
  0.0 84.8 jit_solution(3388176625733208086)
XLA Ops:
  0.6 78.6 %layer.1 = (bf16[1024,512]{1,0:T(8,128)(2,1)}, bf16[256,512]{1,0:T(8,128)(2,1)}, bf16[4,2048,128]{2,1,0:T(8,128)(2,1)}, bf16[4,1536,128]{2,1,0:T(8,128)(2,1)}, f32[8,128]{1,0:T(8,128)}) custom-call(bf16[256,512]{1,0:T(8,128)(2,1)} %bitcast.13, s32[4,64]{1,0:T(4,128)} %bitcast.17, s32[1,1024]{1,0:T(1,128)} %bitcast.15, s32[1,1024]{1,0:T(1,128)} %bitcast.16, ...), custom_call_target="tpu_custom_call" | custom-call | tf_op jit(solution)/shard_map/layer/pallas_call | solution.py:565
  79.2 5.5 %place_results.1 = (bf16[1536,512]{1,0:T(8,128)(2,1)}, bf16[512,512]{1,0:T(8,128)(2,1)}, bf16[1024,512]{1,0:T(8,128)(2,1)}, bf16[512,512]{1,0:T(8,128)(2,1)}, bf...) custom-call(bf16[4,2048,128]{2,1,0:T(8,128)(2,1)} %get-tuple-element.21.edge_, ...), custom_call_target="tpu_custom_call" | custom-call | tf_op jit(solution)/shard_map/place_results/pallas_call | solution.py:510

commit v4 on v3

--- a/solution.py
+++ b/solution.py
@@ -216,8 +216,11 @@
     await_bytes(z_done.at[0:7], z_sems.at[1, 1])
     back = {}
 
+    def columns(h):
+        return slice(256 * h, 256 * h + 256)
+
     def share(h, base, axis, size, stage):
-        part = total.at[pair(h), rows_at(base + axis[0] * size, size)]
+        part = total.at[rows_at(base + axis[0] * size, size), columns(h)]
         for s in (2, 1, 3):
             back[stage, h, s] = post(part, part, (stage, h, s), axis[1][s])
 
@@ -226,7 +229,7 @@
         at = bases[h] + chunk(inner[h], 0, small)
         for j in (2 * h, 2 * h + 1):
             joined = jnp.concatenate([z_done[2 * j + k, 0:piece].astype(F32) for k in both], axis=0)
-            total[j, rows_at(at, small)] = joined.astype(BF16)
+            total[rows_at(at, small), 128 * j : 128 * j + 128] = joined.astype(BF16)
         share(h, bases[h], inner[h], small, 3)
     yield
     for h in both:
@@ -236,7 +239,7 @@
     last = []
 
     def to_sibling(h, s):
-        part = total.at[pair(h), rows_at(core * half + chunk(outer[h], -s, large), large)]
+        part = total.at[rows_at(core * half + chunk(outer[h], -s, large), large), columns(h)]
         last.append(post(part, part, (5, h, s), (x, sibling)))
 
     for h in both:
@@ -278,12 +281,12 @@
 
 def layer_kernel(
     nodes, send_rows, senders, receivers, gain, ngain, lat_in, cot_in, ncot_in, w1_in, w2_in, nw1_in, nw2_in,
-    edge_grad, node_grad, edge_total, node_total, gain_total,
+    edge_grad, node_grad, own_total, table_total, node_total, gain_total,
     lat, cot, ncot, w1, w2, nw1, nw2, others, packed, incoming, far_grad, returned, rim_grad, from_rims,
-    onehot, projected, act, slope, hat, scale, raw_grad, pre_grad, node_partial, edge_terms, node_terms, slots, *rest,
+    onehot, projected, act, slope, hat, scale, raw_grad, pre_grad, node_partial, own_terms, table_terms, node_terms, slots, *rest,
 ):
-    edge_scratch, node_scratch = rest[0:10], rest[10:20]
-    load_sems, far_sems, rim_sems, back_sems, back_rim_sems, gain_sems = rest[20:]
+    own_scratch, table_scratch, node_scratch = rest[0:10], rest[10:20], rest[20:30]
+    load_sems, far_sems, rim_sems, back_sems, back_rim_sems, gain_sems = rest[30:]
     here, x, y, z, core = place()
     edges, width = lat.shape
     count = nodes.shape[0]
@@ -323,11 +326,20 @@
 
     def push(src, dst, sems):
         def one(k, carry):
-            to = lax.rem(here + k, patches)
-            send(src.at[rows_at(to * 16, 16)], dst.at[rows_at(here * 16, 16)], sems.at[0], sems.at[1], to, x)
+            row = lax.rem(y + 2 + k // 2, 4) * 16 + lax.rem(core + k, 2)
+            for s in (4, 3, 5, 2, 6, 1, 7, 0):
+                to = row + ring(z, 8, s) * 2
+
+                def go():
+                    send(src.at[rows_at(to * 16, 16)], dst.at[rows_at(here * 16, 16)], sems.at[0], sems.at[1], to, x)
+
+                if s == 0:
+                    pl.when(to != here)(go)
+                else:
+                    go()
             return carry
 
-        lax.fori_loop(1, patches, one, 0)
+        lax.fori_loop(0, patches // 8, one, 0)
 
     mine = rows_at(here * 16, 16)
     all_but_mine = slice(0, 16 * (patches - 1))
@@ -409,15 +421,17 @@
         if start == 0:
             advance(node_sum)
     all_pre = pre_grad[...]
-    put(edge_terms, 3 * width, mm_tn(act[...], raw_grad[...]))
-    put(edge_terms, 0, mm_tn(lat[...], all_pre))
+    put(own_terms, width, mm_tn(act[...], raw_grad[...]))
+    put(own_terms, 0, mm_tn(lat[...], all_pre))
+    own_sum = reduction(own_terms, own_total, where, own_scratch, pending)
+    advance(own_sum)
     send_sum = mm(one_hot_rows(table_row, rows), all_pre).astype(BF16)
     recv_sum = mm(recv_rows, all_pre).astype(BF16)
-    put(edge_terms, width, mm_tn(nodes[...], send_sum[0:count]) + mm_tn(others[...], send_sum[count:]))
-    put(edge_terms, 2 * width, mm_tn(nodes[...], recv_sum))
-    edge_sum = reduction(edge_terms, edge_total, where, edge_scratch, pending)
-    advance(edge_sum)
-    advance(node_sum)
+    put(table_terms, 0, mm_tn(nodes[...], send_sum[0:count]) + mm_tn(others[...], send_sum[count:]))
+    put(table_terms, width, mm_tn(nodes[...], recv_sum))
+    table_sum = reduction(table_terms, table_total, where, table_scratch, pending)
+    advance(table_sum)
+    advance(own_sum)
     gain_rows = [gain_grad[:, 128 * j : 128 * j + 128] for j in range(width // 128)]
     gain_rows += [node_gain_grad[:, 128 * j : 128 * j + 128] for j in range(width // 128)]
     gain_sum = gain_reduction(jnp.concatenate(gain_rows, axis=0), gain_total, where, slots, gain_sems)
@@ -428,16 +442,19 @@
         send(rim_grad.at[RIM : 2 * RIM], from_rims.at[0:RIM], back_rim_sems.at[0, 0], back_rim_sems.at[1, 0], ahead, x),
         send(rim_grad.at[0:RIM], from_rims.at[RIM : 2 * RIM], back_rim_sems.at[0, 1], back_rim_sems.at[1, 1], behind, x),
     )
-    advance(edge_sum)
+    advance(table_sum)
     far_grad[...] = pack(other_grad[2 * RIM :], True)
     push(far_grad, returned, back_sems)
+    advance(node_sum)
     node_partial[...] += mm_nt(send_sum[0:count], w1[width : 2 * width, :]) + mm_nt(recv_sum, w1[2 * width :, :])
-    advance(node_sum)
     advance(gain_sum)
     returned[mine, :] = far_grad[mine, :]
-    advance(edge_sum)
+    advance(own_sum)
     advance(node_sum)
+    advance(table_sum)
     advance(gain_sum)
+    advance(own_sum)
+    advance(table_sum)
     for copy in back_rims:
         copy.wait_recv()
     await_bytes(returned.at[all_but_mine], back_sems.at[1])
@@ -445,13 +462,13 @@
     node_grad[0:RIM, :] = (nodes_done[0:RIM] + from_rims[0:RIM].astype(F32)).astype(BF16)
     node_grad[RIM : count - RIM, :] = nodes_done[RIM : count - RIM].astype(BF16)
     node_grad[count - RIM : count, :] = (nodes_done[count - RIM :] + from_rims[RIM : 2 * RIM].astype(F32)).astype(BF16)
-    advance(edge_sum)
-    advance(node_sum)
     advance(gain_sum)
-    for _ in range(8):
-        advance(edge_sum)
+    for step in range(8):
         advance(node_sum)
-    advance(gain_sum)
+        advance(own_sum)
+        advance(table_sum)
+        if step == 1:
+            advance(gain_sum)
     for copy in rims + back_rims:
         copy.wait_send()
     await_bytes(packed.at[all_but_mine], far_sems.at[0])
@@ -461,50 +478,34 @@
 
 
 def place_kernel(
-    edge_total, node_total, edge_in, node_in, gains, first, second, nfirst, nsecond, edge_out, node_out, gain_out, ngain_out,
-    edge_in_v, node_in_v, edge_v, rows_v, nfirst_v, nsecond_v, first_v, second_v, in_sems, out_sems,
+    own_total, table_total, node_total, edge_in, node_in, gains, first, second, nfirst, nsecond, edge_out, node_out, gain_out, ngain_out, sems
 ):
     width = first.shape[1]
-    starts = []
-    for k, (src, dst) in enumerate(
-        ((edge_total, edge_in_v), (node_total, node_in_v), (edge_in, edge_v), (node_in, rows_v))
-    ):
-        starts.append(pltpu.make_async_copy(src, dst, in_sems.at[k]))
-        starts[-1].start()
-    ends = []
-
-    def out(src, dst):
-        ends.append(pltpu.make_async_copy(src, dst, out_sems.at[len(ends)]))
-        ends[-1].start()
-
-    def relay(source, first, dst):
-        rows = dst.shape[0]
-        for j in range(width // 128):
-            dst[:, 128 * j : 128 * j + 128] = source[j, first : first + rows, :]
-
+    copies = [
+        pltpu.make_async_copy(src, dst, sems.at[k])
+        for k, (src, dst) in enumerate(
+            (
+                (own_total.at[0:width], first.at[0:width]),
+                (table_total, first.at[width : 3 * width]),
+                (own_total.at[width : 2 * width], second),
+                (node_total.at[0 : 2 * width], nfirst),
+                (node_total.at[2 * width : 3 * width], nsecond),
+                (edge_in, edge_out),
+                (node_in, node_out),
+            )
+        )
+    ]
+    for copy in copies:
+        copy.start()
     for j in range(width // 128):
         cols = slice(128 * j, 128 * j + 128)
         gain_out[cols] = gains[j, :].astype(BF16)
         ngain_out[cols] = gains[4 + j, :].astype(BF16)
-    starts[0].wait()
-    relay(edge_in_v, 0, first_v)
-    out(first_v, first)
-    relay(edge_in_v, 3 * width, second_v)
-    out(second_v, second)
-    starts[1].wait()
-    relay(node_in_v, 0, nfirst_v)
-    out(nfirst_v, nfirst)
-    relay(node_in_v, 2 * width, nsecond_v)
-    out(nsecond_v, nsecond)
-    starts[2].wait()
-    out(edge_v, edge_out)
-    starts[3].wait()
-    out(rows_v, node_out)
-    for copy in ends:
+    for copy in copies:
         copy.wait()
 
 
-def place_results(edge_total, node_total, edge_grad, node_grad, gains):
+def place_results(own_total, table_total, node_total, edge_grad, node_grad, gains):
     width = edge_grad.shape[1]
     anywhere, whole = pl.BlockSpec(memory_space=pl.ANY), pl.BlockSpec(memory_space=VMEM)
     return pl.pallas_call(
@@ -516,23 +517,12 @@
                 edge_grad.shape, node_grad.shape, (width,), (width,),
             )
         ),
-        in_specs=[anywhere] * 4 + [whole],
+        in_specs=[whole] * 6,
         out_specs=(anywhere,) * 6 + (whole,) * 2,
-        scratch_shapes=[
-            VMEM(edge_total.shape, BF16),
-            VMEM(node_total.shape, BF16),
-            VMEM(edge_grad.shape, BF16),
-            VMEM(node_grad.shape, BF16),
-            VMEM((2 * width, width), BF16),
-            VMEM((width, width), BF16),
-            VMEM((3 * width, width), BF16),
-            VMEM((width, width), BF16),
-            pltpu.SemaphoreType.DMA((4,)),
-            pltpu.SemaphoreType.DMA((6,)),
-        ],
-        compiler_params=pltpu.CompilerParams(vmem_limit_bytes=56 * 1024 * 1024),
+        scratch_shapes=[pltpu.SemaphoreType.DMA((7,))],
+        compiler_params=pltpu.CompilerParams(vmem_limit_bytes=16 * 1024 * 1024),
         name="place_results",
-    )(edge_total, node_total, edge_grad, node_grad, gains)
+    )(own_total, table_total, node_total, edge_grad, node_grad, gains)
 
 
 def reduction_scratch(total):
@@ -565,14 +555,15 @@
     return pl.pallas_call(
         layer_kernel,
         out_shape=(
-            jax.ShapeDtypeStruct((edges, width), BF16),
-            jax.ShapeDtypeStruct((count, width), BF16),
-            jax.ShapeDtypeStruct((4, 4 * width, 128), BF16),
-            jax.ShapeDtypeStruct((4, 3 * width, 128), BF16),
-            jax.ShapeDtypeStruct((8, 128), F32),
+            VMEM((edges, width), BF16),
+            VMEM((count, width), BF16),
+            VMEM((2 * width, width), BF16),
+            VMEM((2 * width, width), BF16),
+            VMEM((3 * width, width), BF16),
+            VMEM((8, 128), F32),
         ),
-        in_specs=[whole] * 6 + [anywhere] * 7,
-        out_specs=(whole,) * 5,
+        in_specs=[whole] * 6 + [pl.BlockSpec(memory_space=pltpu.HBM)] * 7,
+        out_specs=(whole,) * 6,
         scratch_shapes=[
             VMEM(lat.shape, BF16),
             VMEM(cot.shape, BF16),
@@ -597,11 +588,13 @@
             VMEM((edges, width), BF16),
             VMEM((edges, width), BF16),
             VMEM((count, width), F32),
-            VMEM((4, 4 * width, 128), BF16),
+            VMEM((4, 2 * width, 128), BF16),
+            VMEM((4, 2 * width, 128), BF16),
             VMEM((4, 3 * width, 128), BF16),
             VMEM((18, 8, 128), F32),
         ]
-        + reduction_scratch(4 * width)
+        + reduction_scratch(2 * width)
+        + reduction_scratch(2 * width)
         + reduction_scratch(3 * width)
         + [dma((7,)), dma((2,)), dma((2, 2)), dma((2,)), dma((2, 2)), dma((2, 4))],
         compiler_params=pltpu.CompilerParams(
@@ -619,12 +612,12 @@
     edge_first, edge_second, edge_gain, node_first, node_second, node_gain,
 ):
     width = edge_first.shape[1]
-    edge_grad, node_grad, edge_total, node_total, gains = layer(
+    edge_grad, node_grad, own_total, table_total, node_total, gains = layer(
         edge_latents[0], edge_cotangent[0], node_latents[0], node_cotangent[0], senders, receivers, send_rows.T,
         edge_first, edge_second, edge_gain, node_first, node_second, node_gain,
     )
     first, second, nfirst, nsecond, edge_grad, node_grad, gain_grad, ngain_grad = place_results(
-        edge_total, node_total, edge_grad, node_grad, gains
+        own_total, table_total, node_total, edge_grad, node_grad, gains
     )
     return (
         edge_grad[None], node_grad[None], first, second, nfirst, nsecond,

time: 85 us -> 81.2 us (0.955)
  Pallas kernels: 84 us -> 80.3 us
    pallas_call x1, Pallas kernels: 5.46 us -> 2.89 us  [place_results(): pl.pallas_call(place_kernel, out_shape=tuple((jax.ShapeDtypeStruct(shape,...]
    pallas_call x1, Pallas kernels: 78.6 us -> 77.4 us  [layer(): pl.pallas_call(layer_kernel, out_shape=(VMEM((edges, width), BF16), VMEM(...]
where the time goes in v4:
time: 81.2 us; the launch traced here: 81.1 us
  Pallas kernels  80.3 us (99%)
    pallas_call x1, Pallas kernels, layer(): pl.pallas_call(layer_kernel, out_shape=(VMEM((edges, width), BF16), VMEM(...  77.4 us
    pallas_call x1, Pallas kernels, place_results(): pl.pallas_call(place_kernel, out_shape=tuple((jax.ShapeDtypeStruct(shape,...  2.89 us

profile of v4, /device:TPU:1, one launch (start us, length us, event | category | flops | bytes accessed | tf_op | source)
XLA Modules:
  0.0 81.1 jit_solution(12502371796827368000)
XLA Ops:
  0.6 77.4 %layer.1 = (bf16[1024,512]{1,0:T(8,128)(2,1)S(1)}, bf16[256,512]{1,0:T(8,128)(2,1)S(1)}, bf16[1024,512]{1,0:T(8,128)(2,1)S(1)}, bf16[1024,512]{1,0:T(8,128)(2,1)...) custom-call(bf16[256,512]{1,0:T(8,128)(2,1)} %bitcast.13, s32[4,64]{1,0:T(4,128)} %bitcast.17, ...), custom_call_target="tpu_custom_call" | custom-call | tf_op jit(solution)/shard_map/layer/pallas_call | solution.py:555
  78.0 2.9 %place_results.1 = (bf16[1536,512]{1,0:T(8,128)(2,1)}, bf16[512,512]{1,0:T(8,128)(2,1)}, bf16[1024,512]{1,0:T(8,128)(2,1)}, bf16[512,512]{1,0:T(8,128)(2,1)}, bf...) custom-call(bf16[1024,512]{1,0:T(8,128)(2,1)S(1)} %get-tuple-element.22.own_t, ...), custom_call_target="tpu_custom_call" | custom-call | tf_op jit(solution)/shard_map/place_results/pallas_call | solution.py:511

commit v5 on v4

--- a/solution.py
+++ b/solution.py
@@ -280,9 +280,9 @@
 
 
 def layer_kernel(
-    nodes, send_rows, senders, receivers, gain, ngain, lat_in, cot_in, ncot_in, w1_in, w2_in, nw1_in, nw2_in,
+    nodes_in, send_rows, senders, receivers, gain, ngain, lat_in, cot_in, ncot_in, w1_in, w2_in, nw1_in, nw2_in,
     edge_grad, node_grad, own_total, table_total, node_total, gain_total,
-    lat, cot, ncot, w1, w2, nw1, nw2, others, packed, incoming, far_grad, returned, rim_grad, from_rims,
+    nodes, lat, cot, ncot, w1, w2, nw1, nw2, others, packed, incoming, far_grad, returned, rim_grad, from_rims,
     onehot, projected, act, slope, hat, scale, raw_grad, pre_grad, node_partial, own_terms, table_terms, node_terms, slots, *rest,
 ):
     own_scratch, table_scratch, node_scratch = rest[0:10], rest[10:20], rest[20:30]
@@ -303,7 +303,10 @@
     loads = [
         pltpu.make_async_copy(src, dst, load_sems.at[k])
         for k, (src, dst) in enumerate(
-            ((w1_in, w1), (lat_in, lat), (w2_in, w2), (nw1_in, nw1), (nw2_in, nw2), (ncot_in, ncot), (cot_in, cot))
+            (
+                (nodes_in, nodes), (w1_in, w1), (lat_in, lat), (w2_in, w2),
+                (nw1_in, nw1), (nw2_in, nw2), (ncot_in, ncot), (cot_in, cot),
+            )
         )
     ]
     for copy in loads:
@@ -317,6 +320,7 @@
     for s in (1, 2, 3):
         signal(here, ring(x, 4, s))
     spread_nodes = send_one_hot(send_rows[...], count)
+    loads[0].wait()
     packed[...] = pack(mm_tn(spread_nodes, nodes[...]).astype(BF16), False)
     pl.semaphore_wait(pltpu.get_barrier_semaphore(), patches + 2)
     rims = (
@@ -324,7 +328,7 @@
         send(nodes.at[0:RIM], others.at[RIM : 2 * RIM], rim_sems.at[0, 1], rim_sems.at[1, 1], behind, x),
     )
 
-    def push(src, dst, sems):
+    def push(src, dst, sems, first, last):
         def one(k, carry):
             row = lax.rem(y + 2 + k // 2, 4) * 16 + lax.rem(core + k, 2)
             for s in (4, 3, 5, 2, 6, 1, 7, 0):
@@ -339,11 +343,11 @@
                     go()
             return carry
 
-        lax.fori_loop(0, patches // 8, one, 0)
+        lax.fori_loop(first, last, one, 0)
 
     mine = rows_at(here * 16, 16)
     all_but_mine = slice(0, 16 * (patches - 1))
-    push(packed, incoming, far_sems)
+    push(packed, incoming, far_sems, 0, patches // 8)
 
     send_row, recv_row = senders[...], receivers[...]
     table_row = jnp.where(send_row < RIM, send_row + count, jnp.where(send_row < RIM + count, send_row - RIM, send_row))
@@ -353,10 +357,10 @@
     onehot[:, count : 2 * count] = one_hot_cols(recv_col, count)
     onehot[:, 2 * count : 2 * count + outside] = one_hot_cols(send_col, outside, count)
     recv_rows = one_hot_rows(recv_row, count)
-    loads[0].wait()
+    loads[1].wait()
     projected[0:count, :] = mm(nodes[...], w1[width : 2 * width, :]).astype(BF16)
     projected[count : 2 * count, :] = mm(nodes[...], w1[2 * width :, :]).astype(BF16)
-    loads[1].wait()
+    loads[2].wait()
     for start in range(0, edges, block):
         part = slice(start, start + block)
         slope[part, :] = mm(lat[part, :], w1[0:width, :]) + mm(onehot[part, 0 : 2 * count], projected[0 : 2 * count, :])
@@ -367,7 +371,7 @@
     await_bytes(incoming.at[all_but_mine], far_sems.at[1])
     others[2 * RIM :, :] = unpack(incoming[...], True)
     projected[2 * count : 2 * count + outside, :] = mm(others[...], w1[width : 2 * width, :]).astype(BF16)
-    loads[2].wait()
+    loads[3].wait()
     edge_gain = gain[...]
     inflow = jnp.zeros((count, width), F32)
     for start in range(0, edges, block):
@@ -382,7 +386,7 @@
         scale[part, :] = inv
         inflow = inflow + mm(recv_rows[:, part], (normed * edge_gain).astype(BF16))
     inflow = inflow.astype(BF16)
-    for copy in loads[3:]:
+    for copy in loads[4:]:
         copy.wait()
     node_pre = mm(nodes[...], nw1[0:width, :]) + mm(inflow, nw1[width:, :])
     node_sig = jax.nn.sigmoid(node_pre)
@@ -443,18 +447,22 @@
         send(rim_grad.at[0:RIM], from_rims.at[RIM : 2 * RIM], back_rim_sems.at[0, 1], back_rim_sems.at[1, 1], behind, x),
     )
     advance(table_sum)
+    advance(node_sum)
     far_grad[...] = pack(other_grad[2 * RIM :], True)
-    push(far_grad, returned, back_sems)
-    advance(node_sum)
     node_partial[...] += mm_nt(send_sum[0:count], w1[width : 2 * width, :]) + mm_nt(recv_sum, w1[2 * width :, :])
     advance(gain_sum)
     returned[mine, :] = far_grad[mine, :]
-    advance(own_sum)
+    for step in (own_sum, node_sum, table_sum, gain_sum, own_sum, table_sum, node_sum):
+        advance(step)
+    parts = patches // 8
+    turns = (own_sum, table_sum, node_sum, own_sum, table_sum, node_sum, own_sum, table_sum)
+    for k, step in enumerate(turns):
+        push(far_grad, returned, back_sems, parts * k // 8, parts * (k + 1) // 8)
+        advance(step)
+        if k == 4:
+            advance(gain_sum)
+    advance(gain_sum)
     advance(node_sum)
-    advance(table_sum)
-    advance(gain_sum)
-    advance(own_sum)
-    advance(table_sum)
     for copy in back_rims:
         copy.wait_recv()
     await_bytes(returned.at[all_but_mine], back_sems.at[1])
@@ -462,13 +470,10 @@
     node_grad[0:RIM, :] = (nodes_done[0:RIM] + from_rims[0:RIM].astype(F32)).astype(BF16)
     node_grad[RIM : count - RIM, :] = nodes_done[RIM : count - RIM].astype(BF16)
     node_grad[count - RIM : count, :] = (nodes_done[count - RIM :] + from_rims[RIM : 2 * RIM].astype(F32)).astype(BF16)
-    advance(gain_sum)
-    for step in range(8):
-        advance(node_sum)
+    for _ in (0, 1):
         advance(own_sum)
         advance(table_sum)
-        if step == 1:
-            advance(gain_sum)
+        advance(node_sum)
     for copy in rims + back_rims:
         copy.wait_send()
     await_bytes(packed.at[all_but_mine], far_sems.at[0])
@@ -562,9 +567,10 @@
             VMEM((3 * width, width), BF16),
             VMEM((8, 128), F32),
         ),
-        in_specs=[whole] * 6 + [pl.BlockSpec(memory_space=pltpu.HBM)] * 7,
+        in_specs=[anywhere] + [whole] * 5 + [anywhere] * 7,
         out_specs=(whole,) * 6,
         scratch_shapes=[
+            VMEM(nodes.shape, BF16),
             VMEM(lat.shape, BF16),
             VMEM(cot.shape, BF16),
             VMEM(ncot.shape, BF16),
@@ -596,7 +602,7 @@
         + reduction_scratch(2 * width)
         + reduction_scratch(2 * width)
         + reduction_scratch(3 * width)
-        + [dma((7,)), dma((2,)), dma((2, 2)), dma((2,)), dma((2, 2)), dma((2, 4))],
+        + [dma((8,)), dma((2,)), dma((2, 2)), dma((2,)), dma((2, 2)), dma((2, 4))],
         compiler_params=pltpu.CompilerParams(
             collective_id=0, has_side_effects=True, vmem_limit_bytes=56 * 1024 * 1024
         ),

time: 81.2 us -> 79.1 us (0.974)
  Pallas kernels: 80.3 us -> 78.3 us
    pallas_call x1, Pallas kernels: 77.4 us -> 75.4 us  [layer(): pl.pallas_call(layer_kernel, out_shape=(VMEM((edges, width), BF16), VMEM(...]
where the time goes in v5:
time: 79.1 us; the launch traced here: 78.9 us
  Pallas kernels  78.3 us (99%)
    pallas_call x1, Pallas kernels, layer(): pl.pallas_call(layer_kernel, out_shape=(VMEM((edges, width), BF16), VMEM(...  75.4 us
    pallas_call x1, Pallas kernels, place_results(): pl.pallas_call(place_kernel, out_shape=tuple((jax.ShapeDtypeStruct(shape,...  2.89 us

profile of v5, /device:TPU:1, one launch (start us, length us, event | category | flops | bytes accessed | tf_op | source)
XLA Modules:
  0.0 78.9 jit_solution(11198642025726945808)
XLA Ops:
  0.6 75.4 %layer.1 = (bf16[1024,512]{1,0:T(8,128)(2,1)S(1)}, bf16[256,512]{1,0:T(8,128)(2,1)S(1)}, bf16[1024,512]{1,0:T(8,128)(2,1)S(1)}, bf16[1024,512]{1,0:T(8,128)(2,1)...) custom-call(bf16[256,512]{1,0:T(8,128)(2,1)} %bitcast.13, s32[4,64]{1,0:T(4,128)} %bitcast.17, ...), custom_call_target="tpu_custom_call" | custom-call | tf_op jit(solution)/shard_map/layer/pallas_call | solution.py:560
  76.1 2.9 %place_results.1 = (bf16[1536,512]{1,0:T(8,128)(2,1)}, bf16[512,512]{1,0:T(8,128)(2,1)}, bf16[1024,512]{1,0:T(8,128)(2,1)}, bf16[512,512]{1,0:T(8,128)(2,1)}, bf...) custom-call(bf16[1024,512]{1,0:T(8,128)(2,1)S(1)} %get-tuple-element.22.own_t, ...), custom_call_target="tpu_custom_call" | custom-call | tf_op jit(solution)/shard_map/place_results/pallas_call | solution.py:516

commit v6 on v5

--- a/solution.py
+++ b/solution.py
@@ -408,7 +408,6 @@
     pending = []
     node_sum = reduction(node_terms, node_total, where, node_scratch, pending)
     advance(node_sum)
-    node_partial[...] = upstream + mm_nt(node_pre_grad, nw1[0:width, :])
     inflow_grad = mm_nt(node_pre_grad, nw1[width:, :]).astype(BF16)
     gain_grad = jnp.zeros((1, width), F32)
     for start in range(0, edges, block):
@@ -421,7 +420,6 @@
         raw_grad[part, :] = back
         pre_back = (mm_nt(back, w2[...]) * slope[part, :]).astype(BF16)
         pre_grad[part, :] = pre_back
-        edge_grad[part, :] = (edge_cot + mm_nt(pre_back, w1[0:width, :])).astype(BF16)
         if start == 0:
             advance(node_sum)
     all_pre = pre_grad[...]
@@ -449,7 +447,11 @@
     advance(table_sum)
     advance(node_sum)
     far_grad[...] = pack(other_grad[2 * RIM :], True)
+    node_partial[...] = upstream + mm_nt(node_pre_grad, nw1[0:width, :])
     node_partial[...] += mm_nt(send_sum[0:count], w1[width : 2 * width, :]) + mm_nt(recv_sum, w1[2 * width :, :])
+    for start in range(0, edges, block):
+        part = slice(start, start + block)
+        edge_grad[part, :] = (cot[part, :].astype(F32) + mm_nt(pre_grad[part, :], w1[0:width, :])).astype(BF16)
     advance(gain_sum)
     returned[mine, :] = far_grad[mine, :]
     for step in (own_sum, node_sum, table_sum, gain_sum, own_sum, table_sum, node_sum):

time: 79.1 us -> 78.8 us (level)
  no operation moved by 1% of the time
where the time goes in v6:
time: 78.8 us; the launch traced here: 78.7 us
  Pallas kernels  77.8 us (99%)
  between operations  0.81 us (1%)
    pallas_call x1, Pallas kernels, layer(): pl.pallas_call(layer_kernel, out_shape=(VMEM((edges, width), BF16), VMEM(...  75 us
    pallas_call x1, Pallas kernels, place_results(): pl.pallas_call(place_kernel, out_shape=tuple((jax.ShapeDtypeStruct(shape,...  2.89 us

profile of v6, /device:TPU:1, one launch (start us, length us, event | category | flops | bytes accessed | tf_op | source)
XLA Modules:
  0.0 78.7 jit_solution(2187853277307399339)
XLA Ops:
  0.6 75.0 %layer.1 = (bf16[1024,512]{1,0:T(8,128)(2,1)S(1)}, bf16[256,512]{1,0:T(8,128)(2,1)S(1)}, bf16[1024,512]{1,0:T(8,128)(2,1)S(1)}, bf16[1024,512]{1,0:T(8,128)(2,1)...) custom-call(bf16[256,512]{1,0:T(8,128)(2,1)} %bitcast.13, s32[4,64]{1,0:T(4,128)} %bitcast.17, ...), custom_call_target="tpu_custom_call" | custom-call | tf_op jit(solution)/shard_map/layer/pallas_call | solution.py:562
  75.6 2.9 %place_results.1 = (bf16[1536,512]{1,0:T(8,128)(2,1)}, bf16[512,512]{1,0:T(8,128)(2,1)}, bf16[1024,512]{1,0:T(8,128)(2,1)}, bf16[512,512]{1,0:T(8,128)(2,1)}, bf...) custom-call(bf16[1024,512]{1,0:T(8,128)(2,1)S(1)} %get-tuple-element.22.own_t, ...), custom_call_target="tpu_custom_call" | custom-call | tf_op jit(solution)/shard_map/place_results/pallas_call | solution.py:518
